TPU v7x, 32 devices: a whole 2x2x4 slice. The times are simulated.
32 devices in a mesh: dp: 8 (over z, y), blk: 4 (over x, core).
Axes of the slice: x: 2, y: 2, z: 4, core: 2. Of those that a mesh axis runs over, the one named last changes fastest.
Arguments:
- long_input: bfloat16 [24, 512, 768], P('dp', 'blk'), may hold values from -6 to 6
- short_input: bfloat16 [8, 4, 8, 128, 768], P('dp', 'blk'), may hold values from -6 to 6
- long_cotan: bfloat16 [24, 512, 768], P('dp', 'blk'), may hold values from -6 to 6
- short_cotan: bfloat16 [8, 4, 8, 128, 768], P('dp', 'blk'), may hold values from -6 to 6
- live_slots: int32 [8, 4], P('dp', 'blk'), may hold values from 1 to 8, as said below
- w_project: bfloat16 [768, 1152], replicated, may hold values from -0.3125 to 0.3125
- bias_query: bfloat16 [384], replicated, may hold values from -3 to 3
- bias_value: bfloat16 [384], replicated, may hold values from -3 to 3
- depth_kernel: bfloat16 [9, 768], replicated, may hold values from -2 to 2
- w_point: bfloat16 [768, 384], replicated, may hold values from -0.21875 to 0.21875
- bias_point: bfloat16 [384], replicated, may hold values from -3 to 3
- w_span: bfloat16 [384, 54], replicated, may hold values from -0.3125 to 0.3125
- bias_span: bfloat16 [54], replicated, may hold values from -3 to 3
- w_unfold: bfloat16 [768, 384], replicated, may hold values from -0.21875 to 0.21875
- bias_unfold: bfloat16 [384], replicated, may hold values from -3 to 3
- w_output: bfloat16 [768, 768], replicated, may hold values from -0.875 to 0.875
- bias_output: bfloat16 [768], replicated, may hold values from -3 to 3
- gain_first: bfloat16 [768], replicated, may hold values from 0.25 to 1.75
- shift_first: bfloat16 [768], replicated, may hold values from -2 to 2
- w_inner: bfloat16 [2, 384, 1536], replicated, may hold values from -0.3125 to 0.3125
- bias_inner: bfloat16 [3072], replicated, may hold values from -3 to 3
- w_outer: bfloat16 [2, 1536, 384], replicated, may hold values from -0.15625 to 0.15625
- bias_outer: bfloat16 [768], replicated, may hold values from -3 to 3
- gain_second: bfloat16 [768], replicated, may hold values from 0.25 to 1.75
- shift_second: bfloat16 [768], replicated, may hold values from -2 to 2
Outputs:
- long_output: bfloat16 [24, 512, 768], P('dp', 'blk')
- short_output: bfloat16 [8, 4, 8, 128, 768], P('dp', 'blk')
- long_grad: float32 [24, 512, 768], P('dp', 'blk')
- short_grad: float32 [8, 4, 8, 128, 768], P('dp', 'blk')
- w_project_grad: float32 [768, 1152], replicated
- bias_query_grad: float32 [384], replicated
- bias_value_grad: float32 [384], replicated
- depth_kernel_grad: float32 [9, 768], replicated
- w_point_grad: float32 [768, 384], replicated
- bias_point_grad: float32 [384], replicated
- w_span_grad: float32 [384, 54], replicated
- bias_span_grad: float32 [54], replicated
- w_unfold_grad: float32 [768, 384], replicated
- bias_unfold_grad: float32 [384], replicated
- w_output_grad: float32 [768, 768], replicated
- bias_output_grad: float32 [768], replicated
- gain_first_grad: float32 [768], replicated
- shift_first_grad: float32 [768], replicated
- w_inner_grad: float32 [2, 384, 1536], replicated
- bias_inner_grad: float32 [3072], replicated
- w_outer_grad: float32 [2, 1536, 384], replicated
- bias_outer_grad: float32 [768], replicated
- gain_second_grad: float32 [768], replicated
- shift_second_grad: float32 [768], replicated
Inputs may be any that keep to these rules, and one draw needn't show every extreme that they name: Device (i, j) uses its short row slots 0 to live_slots[i, j] - 1; in every draw some device uses all 8.
All inputs are finite; a program needn't handle non-finite values.
Results may differ from a plain program's by a relative error of at most 0.014.
The roundings to bfloat16 on the way count: a program that leaves them out, or rounds other values in their place, can miss the bound.
Values may be sent and summed in bfloat16 or wider, within the bound.
A program may use at most 192 MiB of HBM per device.

v0:
```python
import jax
import jax.numpy as jnp
from jax import lax
from jax.sharding import PartitionSpec as P

D = 768
FF = 3072
HEADS = 6
HEAD = 64
KERNEL = 9
GROUPS = 2
ALL = 384


root_half = 0.7071067811865476
density_scale = 0.3989422804014327


def with_halo(block, sides, width):
    for axis, dim in sides:
        count = lax.axis_size(axis)
        forward = [(i, i + 1) for i in range(count - 1)]
        backward = [(target, source) for source, target in forward]
        low = lax.ppermute(
            lax.slice_in_dim(block, block.shape[dim] - width, None, axis=dim), axis, forward
        )
        high = lax.ppermute(lax.slice_in_dim(block, 0, width, axis=dim), axis, backward)
        block = jnp.concatenate([low, block, high], axis=dim)
    return block


def dense(left_side, right_side):
    return jnp.dot(left_side, right_side, preferred_element_type=jnp.float32)


def dense_rows(left_side, right_side):
    return lax.dot_general(
        left_side, right_side, (((0,), (0,)), ((), ())), preferred_element_type=jnp.float32
    )


def dense_back(left_side, right_side):
    return lax.dot_general(
        left_side, right_side, (((1,), (1,)), ((), ())), preferred_element_type=jnp.float32
    )


def column_sum(matrix):
    return jnp.sum(matrix.astype(jnp.float32), axis=0)


def norm_forward(inputs, gain_vector, shift_vector):
    centre = inputs - jnp.mean(inputs, axis=-1, keepdims=True)
    inverse = lax.rsqrt(jnp.mean(centre * centre, axis=-1, keepdims=True) + 1e-12)
    normed = centre * inverse
    return (
        normed * gain_vector.astype(jnp.float32) + shift_vector.astype(jnp.float32),
        normed,
        inverse,
    )


def norm_back(upstream, normed, inverse, gain_vector):
    scaled = upstream * gain_vector.astype(jnp.float32)
    plain_mean = jnp.mean(scaled, axis=-1, keepdims=True)
    cross_mean = jnp.mean(scaled * normed, axis=-1, keepdims=True)
    return (
        inverse * (scaled - plain_mean - normed * cross_mean),
        jnp.sum(upstream * normed, axis=0),
        jnp.sum(upstream, axis=0),
    )


def gelu_slope(inputs):
    return (
        0.5 * (1.0 + lax.erf(inputs * root_half))
        + inputs * jnp.exp(-0.5 * inputs * inputs) * density_scale
    )


def head_split(matrix):
    return matrix.reshape(matrix.shape[0], matrix.shape[1], HEADS, HEAD)


def attend(queries, key_rows, value_rows):
    scores = jnp.einsum(
        "bqhd,bkhd->bhqk",
        head_split(queries),
        head_split(key_rows),
        preferred_element_type=jnp.float32,
    ) * HEAD ** (-0.5)
    weights = jax.nn.softmax(scores, axis=-1).astype(jnp.bfloat16)
    context = jnp.einsum(
        "bhqk,bkhd->bqhd", weights, head_split(value_rows), preferred_element_type=jnp.float32
    )
    return context.reshape(queries.shape).astype(jnp.bfloat16)


def attend_back(queries, key_rows, value_rows, context_grad):
    query_heads = head_split(queries)
    key_heads = head_split(key_rows)
    value_heads = head_split(value_rows)
    grad_heads = head_split(context_grad)
    score_scale = HEAD ** (-0.5)
    scores = (
        jnp.einsum("bqhd,bkhd->bhqk", query_heads, key_heads, preferred_element_type=jnp.float32)
        * score_scale
    )
    weights = jax.nn.softmax(scores, axis=-1)
    weight_grad = jnp.einsum(
        "bqhd,bkhd->bhqk", grad_heads, value_heads, preferred_element_type=jnp.float32
    )
    value_grad = jnp.einsum(
        "bhqk,bqhd->bkhd",
        weights.astype(jnp.bfloat16),
        grad_heads,
        preferred_element_type=jnp.float32,
    )
    score_grad = (
        weights * (weight_grad - jnp.sum(weights * weight_grad, axis=-1, keepdims=True))
    ).astype(jnp.bfloat16)
    query_grad = (
        jnp.einsum("bhqk,bkhd->bqhd", score_grad, key_heads, preferred_element_type=jnp.float32)
        * score_scale
    )
    key_grad = (
        jnp.einsum("bhqk,bqhd->bkhd", score_grad, query_heads, preferred_element_type=jnp.float32)
        * score_scale
    )
    return (
        query_grad.reshape(queries.shape),
        key_grad.reshape(key_rows.shape),
        value_grad.reshape(value_rows.shape),
    )


def conv_forward(padded, queries, valid, conv_weights):
    depth_kernel, w_point, bias_point, w_span, bias_span, w_unfold, bias_unfold = conv_weights
    batch_rows, seq_length = (queries.shape[0], queries.shape[1])
    widened = padded.astype(jnp.float32)
    depth_sum = sum(
        (
            depth_kernel[offset].astype(jnp.float32) * widened[:, offset : offset + seq_length]
            for offset in range(KERNEL)
        )
    )
    depth_low = depth_sum.astype(jnp.bfloat16).reshape(-1, D)
    key_conv = dense(depth_low, w_point) + bias_point
    span_low = (key_conv * queries.reshape(-1, ALL).astype(jnp.float32)).astype(jnp.bfloat16)
    logits = (dense(span_low, w_span) + bias_span).reshape(batch_rows, seq_length, HEADS, KERNEL)
    kernel = jax.nn.softmax(logits, axis=-1)
    unfold_rows = (dense(padded.reshape(-1, D), w_unfold) + bias_unfold).reshape(
        batch_rows, seq_length + KERNEL - 1, HEADS, HEAD
    ) * valid[None, :, None, None]
    conv_rows = sum(
        (
            kernel[:, :, :, offset, None] * unfold_rows[:, offset : offset + seq_length]
            for offset in range(KERNEL)
        )
    )
    kept_values = (widened, depth_low, key_conv, span_low, kernel, unfold_rows)
    return (conv_rows.reshape(batch_rows, seq_length, ALL).astype(jnp.bfloat16), kept_values)


def conv_back(queries, kept_values, conv_grad, conv_weights):
    depth_kernel, w_point, bias_point, w_span, bias_span, w_unfold, bias_unfold = conv_weights
    widened, depth_low, key_conv, span_low, kernel, unfold_rows = kept_values
    batch_rows, seq_length = (queries.shape[0], queries.shape[1])
    reach_width = KERNEL - 1
    grad_heads = conv_grad.astype(jnp.float32).reshape(batch_rows, seq_length, HEADS, HEAD)
    kernel_grad = jnp.stack(
        [
            jnp.sum(grad_heads * unfold_rows[:, offset : offset + seq_length], axis=-1)
            for offset in range(KERNEL)
        ],
        axis=-1,
    )
    unfold_grad = sum(
        (
            jnp.pad(
                kernel[:, :, :, offset, None] * grad_heads,
                ((0, 0), (offset, reach_width - offset), (0, 0), (0, 0)),
            )
            for offset in range(KERNEL)
        )
    )
    logit_grad = kernel * (kernel_grad - jnp.sum(kernel * kernel_grad, axis=-1, keepdims=True))
    logit_low = logit_grad.reshape(-1, HEADS * KERNEL).astype(jnp.bfloat16)
    span_grad = dense_back(logit_low, w_span)
    point_low = (span_grad * queries.reshape(-1, ALL).astype(jnp.float32)).astype(jnp.bfloat16)
    query_grad = span_grad * key_conv
    depth_grad = dense_back(point_low, w_point).reshape(batch_rows, seq_length, D)
    kernel_weight_grad = jnp.stack(
        [
            jnp.sum(depth_grad * widened[:, offset : offset + seq_length], axis=(0, 1))
            for offset in range(KERNEL)
        ],
        axis=0,
    )
    pad_grad = sum(
        (
            jnp.pad(
                depth_kernel[offset].astype(jnp.float32) * depth_grad,
                ((0, 0), (offset, reach_width - offset), (0, 0)),
            )
            for offset in range(KERNEL)
        )
    )
    weight_grads = (
        kernel_weight_grad,
        dense_rows(depth_low, point_low),
        column_sum(point_low),
        dense_rows(span_low, logit_low),
        column_sum(logit_low),
    )
    return (
        query_grad,
        unfold_grad.reshape(batch_rows, seq_length + reach_width, ALL),
        pad_grad,
        weight_grads,
    )


def shards(
    long_input,
    short_input,
    long_cotan,
    short_cotan,
    live_slots,
    w_project,
    bias_query,
    bias_value,
    depth_kernel,
    w_point,
    bias_point,
    w_span,
    bias_span,
    w_unfold,
    bias_unfold,
    w_output,
    bias_output,
    gain_first,
    shift_first,
    w_inner,
    bias_inner,
    w_outer,
    bias_outer,
    gain_second,
    shift_second,
):
    batch_rows, segment = (long_input.shape[0], long_input.shape[1])
    slot_count, short_length = (short_input.shape[2], short_input.shape[3])
    reach_width = KERNEL - 1
    half_width = reach_width // 2
    long_count = batch_rows * segment
    short_rows = short_input[0, 0]
    conv_weights = (depth_kernel, w_point, bias_point, w_span, bias_span, w_unfold, bias_unfold)
    long_pad = with_halo(long_input, (("blk", 1),), half_width)
    short_pad = jnp.pad(short_rows, ((0, 0), (half_width, half_width), (0, 0)))
    position = lax.axis_index("blk")
    blk_count = lax.axis_size("blk")
    long_edge = jnp.arange(segment + reach_width)
    lower_valid = jnp.logical_or(long_edge >= half_width, position > 0)
    upper_valid = jnp.logical_or(long_edge < segment + half_width, position < blk_count - 1)
    long_valid = jnp.logical_and(lower_valid, upper_valid).astype(jnp.float32)
    short_edge = jnp.arange(short_length + reach_width)
    short_valid = jnp.logical_and(
        short_edge >= half_width, short_edge < short_length + half_width
    ).astype(jnp.float32)
    tokens = jnp.concatenate([long_input.reshape(-1, D), short_rows.reshape(-1, D)], axis=0)
    token_count = tokens.shape[0]
    project = dense(tokens, w_project)
    queries = (project[:, :ALL] + bias_query).astype(jnp.bfloat16)
    key_rows = project[:, ALL : 2 * ALL].astype(jnp.bfloat16)
    value_rows = (project[:, 2 * ALL :] + bias_value).astype(jnp.bfloat16)
    long_shape = (batch_rows, segment, ALL)
    short_shape = (slot_count, short_length, ALL)
    long_queries = queries[:long_count].reshape(long_shape)
    short_queries = queries[long_count:].reshape(short_shape)
    long_keys = key_rows[:long_count].reshape(long_shape)
    short_keys = key_rows[long_count:].reshape(short_shape)
    long_values = value_rows[:long_count].reshape(long_shape)
    short_values = value_rows[long_count:].reshape(short_shape)
    full_keys, full_values = (
        lax.all_gather(long_keys, "blk", axis=1, tiled=True),
        lax.all_gather(long_values, "blk", axis=1, tiled=True),
    )
    long_context = attend(long_queries, full_keys, full_values)
    short_context = attend(short_queries, short_keys, short_values)
    long_conv, long_kept = conv_forward(long_pad, long_queries, long_valid, conv_weights)
    short_conv, short_kept = conv_forward(short_pad, short_queries, short_valid, conv_weights)
    context_rows = jnp.concatenate(
        [long_context.reshape(-1, ALL), short_context.reshape(-1, ALL)], axis=0
    )
    conv_rows = jnp.concatenate([long_conv.reshape(-1, ALL), short_conv.reshape(-1, ALL)], axis=0)
    mixed_rows = jnp.concatenate([context_rows, conv_rows], axis=1)
    attended = dense(mixed_rows, w_output) + bias_output
    first_norm, first_normed, first_inverse = norm_forward(
        attended + tokens.astype(jnp.float32), gain_first, shift_first
    )
    first_low = first_norm.astype(jnp.bfloat16).reshape(token_count, GROUPS, D // GROUPS)
    inner_sum = (
        jnp.einsum("ngi,gio->ngo", first_low, w_inner, preferred_element_type=jnp.float32).reshape(
            token_count, FF
        )
        + bias_inner
    )
    active = (
        jax.nn.gelu(inner_sum, approximate=False)
        .astype(jnp.bfloat16)
        .reshape(token_count, GROUPS, FF // GROUPS)
    )
    outer_sum = (
        jnp.einsum("ngi,gio->ngo", active, w_outer, preferred_element_type=jnp.float32).reshape(
            token_count, D
        )
        + bias_outer
    )
    output_rows, second_normed, second_inverse = norm_forward(
        outer_sum + first_norm, gain_second, shift_second
    )
    output_low = output_rows.astype(jnp.bfloat16)
    long_output = output_low[:long_count].reshape(long_input.shape)
    short_output = output_low[long_count:].reshape(short_input.shape)
    live_mask = (jnp.arange(slot_count) < live_slots[0, 0]).astype(jnp.float32)
    short_seed = short_cotan[0, 0].astype(jnp.float32) * live_mask[:, None, None]
    upstream = jnp.concatenate(
        [long_cotan.reshape(-1, D).astype(jnp.float32), short_seed.reshape(-1, D)], axis=0
    )
    second_grad, gain_second_grad, shift_second_grad = norm_back(
        upstream, second_normed, second_inverse, gain_second
    )
    outer_low = second_grad.astype(jnp.bfloat16)
    bias_outer_grad = column_sum(outer_low)
    outer_groups = outer_low.reshape(token_count, GROUPS, D // GROUPS)
    w_outer_grad = jnp.einsum(
        "ngi,ngo->gio", active, outer_groups, preferred_element_type=jnp.float32
    )
    active_grad = jnp.einsum(
        "ngo,gio->ngi", outer_groups, w_outer, preferred_element_type=jnp.float32
    ).reshape(token_count, FF)
    inner_low = (active_grad * gelu_slope(inner_sum)).astype(jnp.bfloat16)
    bias_inner_grad = column_sum(inner_low)
    inner_groups = inner_low.reshape(token_count, GROUPS, FF // GROUPS)
    w_inner_grad = jnp.einsum(
        "ngi,ngo->gio", first_low, inner_groups, preferred_element_type=jnp.float32
    )
    first_grad = second_grad + jnp.einsum(
        "ngo,gio->ngi", inner_groups, w_inner, preferred_element_type=jnp.float32
    ).reshape(token_count, D)
    (
        w_inner_grad,
        bias_inner_grad,
        w_outer_grad,
        bias_outer_grad,
        gain_second_grad,
        shift_second_grad,
    ) = lax.psum(
        (
            w_inner_grad,
            bias_inner_grad,
            w_outer_grad,
            bias_outer_grad,
            gain_second_grad,
            shift_second_grad,
        ),
        ("dp", "blk"),
    )
    first_in_grad, gain_first_grad, shift_first_grad = norm_back(
        first_grad, first_normed, first_inverse, gain_first
    )
    attended_low = first_in_grad.astype(jnp.bfloat16)
    bias_output_grad = column_sum(attended_low)
    w_output_grad = dense_rows(mixed_rows, attended_low)
    mixed_grad = dense_back(attended_low, w_output)
    context_low = mixed_grad[:, :ALL].astype(jnp.bfloat16)
    conv_low = mixed_grad[:, ALL:].astype(jnp.bfloat16)
    back_keys, back_values = (full_keys, full_values)
    long_query_grad, long_key_part, long_value_part = attend_back(
        long_queries, back_keys, back_values, context_low[:long_count].reshape(long_shape)
    )
    long_key_grad, long_value_grad = (
        lax.psum_scatter(
            long_key_part.astype(jnp.bfloat16), "blk", scatter_dimension=1, tiled=True
        ).astype(jnp.float32),
        lax.psum_scatter(
            long_value_part.astype(jnp.bfloat16), "blk", scatter_dimension=1, tiled=True
        ).astype(jnp.float32),
    )
    short_query_grad, short_key_grad, short_value_grad = attend_back(
        short_queries, short_keys, short_values, context_low[long_count:].reshape(short_shape)
    )
    long_conv_query, long_unfold, long_depth, long_weights = conv_back(
        long_queries, long_kept, conv_low[:long_count].reshape(long_shape), conv_weights
    )
    short_conv_query, short_unfold, short_depth, short_weights = conv_back(
        short_queries, short_kept, conv_low[long_count:].reshape(short_shape), conv_weights
    )
    rim_stack = jnp.concatenate([long_unfold, long_depth], axis=-1)
    rim_pair = jnp.concatenate(
        [rim_stack[:, :half_width], rim_stack[:, segment + half_width :]], axis=1
    )
    received = with_halo(rim_pair.astype(jnp.bfloat16), (("blk", 1),), half_width).astype(
        rim_pair.dtype
    )
    long_core = rim_stack[:, half_width : segment + half_width]
    long_core = long_core + jnp.pad(
        received[:, :half_width], ((0, 0), (0, segment - half_width), (0, 0))
    )
    long_core = long_core + jnp.pad(
        received[:, 3 * half_width :], ((0, 0), (segment - half_width, 0), (0, 0))
    )
    short_core = jnp.concatenate([short_unfold, short_depth], axis=-1)[
        :, half_width : short_length + half_width
    ]
    core_rows = jnp.concatenate(
        [long_core.reshape(-1, ALL + D), short_core.reshape(-1, ALL + D)], axis=0
    )
    unfold_low = core_rows[:, :ALL].astype(jnp.bfloat16)
    bias_unfold_grad = column_sum(unfold_low)
    w_unfold_grad = dense_rows(tokens, unfold_low)
    query_total = jnp.concatenate(
        [
            long_query_grad.reshape(-1, ALL) + long_conv_query,
            short_query_grad.reshape(-1, ALL) + short_conv_query,
        ],
        axis=0,
    )
    key_total = jnp.concatenate(
        [long_key_grad.reshape(-1, ALL), short_key_grad.reshape(-1, ALL)], axis=0
    )
    value_total = jnp.concatenate(
        [long_value_grad.reshape(-1, ALL), short_value_grad.reshape(-1, ALL)], axis=0
    )
    project_low = jnp.concatenate([query_total, key_total, value_total], axis=1).astype(
        jnp.bfloat16
    )
    bias_query_grad = column_sum(project_low[:, :ALL])
    bias_value_grad = column_sum(project_low[:, 2 * ALL :])
    w_project_grad = dense_rows(tokens, project_low)
    token_grad = (
        first_in_grad
        + core_rows[:, ALL:]
        + dense_back(unfold_low, w_unfold)
        + dense_back(project_low, w_project)
    )
    long_grad = token_grad[:long_count].reshape(long_input.shape)
    short_grad = token_grad[long_count:].reshape(short_input.shape)
    depth_kernel_grad = long_weights[0] + short_weights[0]
    w_point_grad = long_weights[1] + short_weights[1]
    bias_point_grad = long_weights[2] + short_weights[2]
    w_span_grad = long_weights[3] + short_weights[3]
    bias_span_grad = long_weights[4] + short_weights[4]
    (
        w_project_grad,
        bias_query_grad,
        bias_value_grad,
        depth_kernel_grad,
        w_point_grad,
        bias_point_grad,
        w_span_grad,
        bias_span_grad,
        w_unfold_grad,
        bias_unfold_grad,
        w_output_grad,
        bias_output_grad,
        gain_first_grad,
        shift_first_grad,
    ) = lax.psum(
        (
            w_project_grad,
            bias_query_grad,
            bias_value_grad,
            depth_kernel_grad,
            w_point_grad,
            bias_point_grad,
            w_span_grad,
            bias_span_grad,
            w_unfold_grad,
            bias_unfold_grad,
            w_output_grad,
            bias_output_grad,
            gain_first_grad,
            shift_first_grad,
        ),
        ("dp", "blk"),
    )
    return (
        long_output,
        short_output,
        long_grad,
        short_grad,
        w_project_grad,
        bias_query_grad,
        bias_value_grad,
        depth_kernel_grad,
        w_point_grad,
        bias_point_grad,
        w_span_grad,
        bias_span_grad,
        w_unfold_grad,
        bias_unfold_grad,
        w_output_grad,
        bias_output_grad,
        gain_first_grad,
        shift_first_grad,
        w_inner_grad,
        bias_inner_grad,
        w_outer_grad,
        bias_outer_grad,
        gain_second_grad,
        shift_second_grad,
    )


def solution(mesh):
    in_specs = (
        P("dp", "blk", None),
        P("dp", "blk", None, None, None),
        P("dp", "blk", None),
        P("dp", "blk", None, None, None),
        P("dp", "blk"),
        P(),
        P(),
        P(),
        P(),
        P(),
        P(),
        P(),
        P(),
        P(),
        P(),
        P(),
        P(),
        P(),
        P(),
        P(),
        P(),
        P(),
        P(),
        P(),
        P(),
    )
    out_specs = (
        P("dp", "blk", None),
        P("dp", "blk", None, None, None),
        P("dp", "blk", None),
        P("dp", "blk", None, None, None),
        P(),
        P(),
        P(),
        P(),
        P(),
        P(),
        P(),
        P(),
        P(),
        P(),
        P(),
        P(),
        P(),
        P(),
        P(),
        P(),
        P(),
        P(),
        P(),
        P(),
    )
    return jax.shard_map(shards, mesh=mesh, in_specs=in_specs, out_specs=out_specs, check_vma=False)
```

profile of v0, /device:TPU:1, one launch (start us, length us, event | category | flops | bytes accessed | tf_op | source)
XLA Modules:
  0.0 791.1 jit_solution(13414145175357089657)
XLA Ops:
  7.3 7.9 %fusion.110 = (bf16[1408,1152]{1,0:T(8,128)(2,1)S(1)}, f32[1408,1152]{1,0:T(8,128)}) fusion(bf16[768,1152]{1,0:T(8,128)(2,1)} %param.30, bf16[1024,768]{1,0:T(8,128)(2,1)} %bitcast.410, bf16[384,768]{1,0:T(8,128)(2,1)} %bitcast.445), kind=kOutput, calls=%fused_computation.345 | convolution fusion | flops 2497363968 | bytes 13664256 | tf_op jit(solution)/shard_map/dot_general | solution.py:33
  51.1 14.7 %add_convert_fusion.1 = bf16[8,128,768]{2,1,0:T(8,128)(2,1)S(1)} fusion(f32[8,136,768]{2,1,0:T(8,128)} %get-tuple-element.158, f32[768]{0:T(1024)S(1)} %get-tuple-element.74, f32[768]{0:T(1024)S(1)} %get-tuple-element.75, f32[768]{0:T(1024)S(1)} %get-tuple-element.68, f32[768]{0:T(1024)S(1)} %get-tuple-element.69, f32[768]{0:T(1024)S(1)} %get-tuple-element.70, ...), kind=kLoop, calls=%fused_computation.87 | loop fusion | flops 14155776 | bytes 29912064 | tf_op jit(solution)/shard_map/convert_element_type | solution.py:147
  145.9 4.9 fusion.112
  168.1 44.4 %fusion.4 = (bf16[1408,2,1536]{2,0,1:T(8,128)(2,1)}, f32[2,1408,1536]{2,1,0:T(8,128)}) fusion(f32[2,1536]{1,0:T(2,128)S(1)} %copy-done.204, bf16[1408,2,384]{0,2,1:T(8,128)(2,1)} %bitcast.357, bf16[2,384,1536]{2,1,0:T(8,128)(2,1)S(1)} %copy-done), kind=kOutput, calls=%fused_computation.6 | convolution fusion | flops 3607363584 | bytes 30486528 | tf_op jit(solution)/shard_map/ngi,gio->ngo/dot_general | solution.py:303
  212.5 9.4 %fusion.114 = f32[2,1408,384]{1,2,0:T(8,128)} fusion(bf16[1408,2,1536]{2,0,1:T(8,128)(2,1)} %get-tuple-element.204, bf16[2,1536,384]{2,1,0:T(8,128)(2,1)S(1)} %copy-done.240), kind=kOutput, calls=%fused_computation.349 | convolution fusion | flops 3321888768 | bytes 15335424 | tf_op jit(solution)/shard_map/ngi,gio->ngo/dot_general | solution.py:314
  221.8 5.8 copy.352
  227.7 4.9 fusion.107
  237.5 4.9 convert_reduce_fusion.1
  242.4 6.9 fusion.37
  249.3 14.0 %convert_reduce_fusion = (f32[2,1536]{1,0:T(2,128)}, bf16[1408,2,1536]{2,0,1:T(8,128)(2,1)S(1)}) fusion(f32[2,1408,1536]{2,1,0:T(8,128)} %get-tuple-element.205, f32[2,1536]{1,0:T(2,128)S(1)} %copy-done.204, bf16[2,1536,384]{2,1,0:T(8,128)(2,1)S(1)} %copy-done.241, bf16[176,2,8,384]{3,2,1,0:T(8,128)(2,1)S(1)} %bitcast.404), kind=kOutput, calls=%fused_computation.20 | convolution fusion | flops 3378115584 | bytes 30498816 | tf_op jit(solution)/shard_map/ngo,gio->ngi/dot_general | solution.py:339
  263.3 5.4 fusion.115
  268.7 5.8 copy.353
  274.6 6.7 multiply_reduce_fusion.2
  319.8 15.6 %broadcast_multiply_fusion.28 = (f32[3,128,6,64]{3,2,1,0:T(8,128)}, f32[3,128,6,64]{3,2,1,0:T(8,128)}, f32[3,128,6,64]{3,2,1,0:T(8,128)}, f32[3,128,6,64]{3,2,1,...) fusion(f32[3,128,6,64]{3,2,1,0:T(8,128)S(1)} %reshape.405, ...), kind=kLoop, calls=%fused_computation.212 | loop fusion | flops 3960576 | bytes 11372544 | tf_op jit(solution)/shard_map/mul | solution.py:181
  361.5 9.1 %multiply_reduce_fusion.22 = (f32[8,128,6]{1,0,2:T(8,128)}, f32[8,128,6]{1,0,2:T(8,128)}, f32[8,128,6]{1,0,2:T(8,128)}, f32[8,128,6]{1,0,2:T(8,128)}, f32[8,128,...) fusion(f32[8,128,6,64]{1,0,3,2:T(8,128)} %bitcast.371, ...), kind=kLoop, calls=%fused_computation.127 | loop fusion | flops 10561536 | bytes 30326784 | tf_op jit(solution)/shard_map/reduce_sum | solution.py:173
  396.5 7.8 pad_add_fusion.1
  415.8 5.6 multiply_reduce_fusion.11
  421.4 8.6 %broadcast_multiply_fusion.9 = (f32[8,128,768]{2,1,0:T(8,128)S(1)}, f32[8,128,768]{2,1,0:T(8,128)}, f32[8,128,768]{2,1,0:T(8,128)}, f32[8,128,768]{2,1,0:T(8,128...) fusion(f32[8,128,768]{2,1,0:T(8,128)S(1)} %bitcast.390, ...), kind=kLoop, calls=%fused_computation.155 | loop fusion | flops 7077888 | bytes 31484928 | tf_op jit(solution)/shard_map/mul | solution.py:203
  430.1 9.7 %pad_add_fusion = f32[8,136,768]{2,1,0:T(8,128)S(1)} fusion(f32[8,128,768]{2,1,0:T(8,128)} %get-tuple-element.118, f32[8,128,768]{2,1,0:T(8,128)} %get-tuple-element.119, f32[8,128,768]{2,1,0:T(8,128)} %get-tuple-element.120, f32[8,128,768]{2,1,0:T(8,128)} %get-tuple-element.121, f32[8,128,768]{2,1,0:T(8,128)} %get-tuple-element.122, ...), kind=kLoop, calls=%fused_computation.70 | loop fusion | flops 6684672 | bytes 31653888 | tf_op jit(solution)/shard_map/add | solution.py:200
  442.5 9.0 %fusion.118 = f32[2,384,1536]{2,1,0:T(8,128)} fusion(bf16[1408,2,384]{0,2,1:T(8,128)(2,1)S(1)} %bitcast.358, bf16[1408,2,1536]{2,0,1:T(8,128)(2,1)} %copy-done.16), kind=kOutput, calls=%fused_computation.353 | convolution fusion | flops 3321888768 | bytes 15532032 | tf_op jit(solution)/shard_map/ngi,ngo->gio/dot_general | solution.py:345
  462.9 7.5 fusion.98
  478.1 7.3 fusion.103
  492.6 44.0 %all-reduce.39 = (f32[384]{0:T(512)}, f32[384]{0:T(512)}, f32[9,768]{1,0:T(8,128)}, f32[384]{0:T(512)}, f32[54]{0:T(128)}, /*index=5*/f32[384]{0:T(512)}, f32[76...) all-reduce(f32[384]{0:T(512)S(1)} %convert_reduce_fusion.5, ...), channel_id=1, replica_groups=mesh['dp'=8,'blk'=4] {'dp','blk'}, use_global_device_ids=true, to_apply=%region_42.43 | all-reduce | flops 16182 | bytes 129456 | tf_op jit(solution)/shard_map/psum | solution.py:469
  536.6 232.5 %all-reduce.43.cloned.1.call-done = (f32[768,1152]{1,0:T(8,128)}, f32[768,384]{1,0:T(8,128)}, f32[384,54]{0,1:T(8,128)}, f32[768,384]{1,0:T(8,128)}, f32[768,768...) async-done(((f32[768,1152]{1,0:T(8,128)}, f32[768,384]{1,0:T(8,128)}, f32[384,54]{0,1:T(8,128)}, f32[768,384]{1,0:T(8,128)}, f32[768,768]{1,0:T(8,128)}, ...) | async-done | bytes 17777680 | tf_op jit(solution)/shard_map/psum | solution.py:469
  (789 shorter events, 280.7 us)
Async XLA Ops:
  7.2 160.8 %copy-start = (bf16[2,384,1536]{2,1,0:T(8,128)(2,1)S(1)}, bf16[2,384,1536]{2,1,0:T(8,128)(2,1)}, u32[]{:S(2)}) copy-start(bf16[2,384,1536]{2,1,0:T(8,128)(2,1)} %param.44) | copy-start | bytes 7077892
  7.2 137.1 %all-gather.5.cloned.1.call-start = ((), (), s32[]{:S(2)}) async-start(), calls=%async_computation.3 | async-start | bytes 1474560 | tf_op jit(solution)/shard_map/all_gather | solution.py:285
  7.3 18.3 %copy-start.234 = (bf16[384]{0:T(512)(128)(2,1)S(1)}, bf16[384]{0:T(512)(128)(2,1)}, u32[]{:S(2)}) copy-start(bf16[384]{0:T(512)(128)(2,1)} %param.32) | copy-start | bytes 2308
  17.7 133.2 %all-gather.3.cloned.1.call-start = ((), (), s32[]{:S(2)}) async-start(), calls=%async_computation.2 | async-start | bytes 1474560 | tf_op jit(solution)/shard_map/all_gather | solution.py:286
  19.1 99.1 %collective-permute-start = (bf16[3,4,768]{2,1,0:T(4,128)(2,1)}, bf16[3,4,768]{2,1,0:T(4,128)(2,1)}, u32[]{:S(2)}, u32[]{:S(2)}) collective-permute-start(bf16[3,4,768]{2,1,0:T(4,128)(2,1)} %get-tuple-element.174), channel_id=1, source_target_pairs={{0,1},{1,2},{2,3},{4,5},{5,6},{6,7},{8,9},{9,10},{10,11},{12,13},{... | collective-permute-start | bytes 55304 | tf_op jit(solution)/shard_map/ppermute | solution.py:24
  23.7 94.6 %collective-permute-start.1 = (bf16[3,4,768]{2,1,0:T(4,128)(2,1)}, bf16[3,4,768]{2,1,0:T(4,128)(2,1)}, u32[]{:S(2)}, u32[]{:S(2)}) collective-permute-start(bf16[3,4,768]{2,1,0:T(4,128)(2,1)} %get-tuple-element.175), channel_id=1, source_target_pairs={{1,0},{2,1},{3,2},{5,4},{6,5},{7,6},{9,8},{10,9},{11,10},{13,12},{... | collective-permute-start | bytes 55304 | tf_op jit(solution)/shard_map/ppermute | solution.py:27
  28.4 94.6 %copy-start.12 = (bf16[1408,384]{1,0:T(8,128)(2,1)}, bf16[1408,384]{1,0:T(8,128)(2,1)S(1)}, u32[]{:S(2)}) copy-start(bf16[1408,384]{1,0:T(8,128)(2,1)S(1)} %get-tuple-element.115) | copy-start | bytes 3244036
  30.2 432.8 %reduce-scatter.5.cloned.1.call-start = ((), (), s32[]{:S(2)}) async-start(), calls=%async_computation.5 | async-start | bytes 1474560 | tf_op jit(solution)/shard_map/reduce_scatter | solution.py:386
  35.7 31.2 %copy-start.223 = (f32[54]{0:T(128)}, f32[54]{0:T(128)S(1)}, u32[]{:S(2)}) copy-start(f32[54]{0:T(128)S(1)} %convert_element_type.499) | copy-start | bytes 652
  35.7 30.1 %copy-start.209 = (f32[384]{0:T(512)}, f32[384]{0:T(512)S(1)}, u32[]{:S(2)}) copy-start(f32[384]{0:T(512)S(1)} %convert_element_type.496) | copy-start | bytes 4612
  36.9 83.4 %copy-start.147 = (f32[768]{0:T(1024)}, f32[768]{0:T(1024)S(1)}, u32[]{:S(2)}) copy-start(f32[768]{0:T(1024)S(1)} %get-tuple-element.67) | copy-start | bytes 9220
  37.0 83.4 %copy-start.149 = (f32[768]{0:T(1024)}, f32[768]{0:T(1024)S(1)}, u32[]{:S(2)}) copy-start(f32[768]{0:T(1024)S(1)} %get-tuple-element.68) | copy-start | bytes 9220
  37.0 83.4 %copy-start.151 = (f32[768]{0:T(1024)}, f32[768]{0:T(1024)S(1)}, u32[]{:S(2)}) copy-start(f32[768]{0:T(1024)S(1)} %get-tuple-element.69) | copy-start | bytes 9220
  37.0 83.4 %copy-start.154 = (f32[768]{0:T(1024)}, f32[768]{0:T(1024)S(1)}, u32[]{:S(2)}) copy-start(f32[768]{0:T(1024)S(1)} %get-tuple-element.70) | copy-start | bytes 9220
  71.0 41.5 %copy-start.116 = (f32[8,128,6]{1,0,2:T(8,128)}, f32[8,128,6]{1,0,2:T(8,128)S(1)}, u32[]{:S(2)}) copy-start(f32[8,128,6]{1,0,2:T(8,128)S(1)} %reduce_max.41) | copy-start | bytes 73732
  72.0 39.8 %copy-start.118 = (f32[8,128,6]{1,0,2:T(8,128)}, f32[8,128,6]{1,0,2:T(8,128)S(1)}, u32[]{:S(2)}) copy-start(f32[8,128,6]{1,0,2:T(8,128)S(1)} %fusion.79) | copy-start | bytes 73732
  73.7 24.9 %copy-start.131 = (f32[8,128,6]{1,0,2:T(8,128)}, f32[8,128,6]{1,0,2:T(8,128)S(1)}, u32[]{:S(2)}) copy-start(f32[8,128,6]{1,0,2:T(8,128)S(1)} %get-tuple-element.176) | copy-start | bytes 73732
  73.7 24.9 %copy-start.133 = (f32[8,128,6]{1,0,2:T(8,128)}, f32[8,128,6]{1,0,2:T(8,128)S(1)}, u32[]{:S(2)}) copy-start(f32[8,128,6]{1,0,2:T(8,128)S(1)} %get-tuple-element.177) | copy-start | bytes 73732
  168.0 44.4 %copy-start.240 = (bf16[2,1536,384]{2,1,0:T(8,128)(2,1)S(1)}, bf16[2,1536,384]{2,1,0:T(8,128)(2,1)}, u32[]{:S(2)}) copy-start(bf16[2,1536,384]{2,1,0:T(8,128)(2,1)} %param.46) | copy-start | bytes 7077892
  319.8 25.2 %copy-start.67 = (f32[3,128,6,9]{1,0,3,2:T(4,128)S(1)}, f32[3,128,6,9]{1,0,3,2:T(4,128)}, u32[]{:S(2)}) copy-start(f32[3,128,6,9]{1,0,3,2:T(4,128)} %copy-done.66) | copy-start | bytes 248836
  355.6 107.3 %reduce-scatter.3.cloned.1.call-start = ((), (), s32[]{:S(2)}) async-start(), calls=%async_computation.4 | async-start | bytes 1474560 | tf_op jit(solution)/shard_map/reduce_scatter | solution.py:383
  410.1 46.2 %collective-permute-start.2 = (bf16[3,4,1152]{2,1,0:T(4,128)(2,1)}, bf16[3,4,1152]{2,1,0:T(4,128)(2,1)}, u32[]{:S(2)}, u32[]{:S(2)}) collective-permute-start(bf16[3,4,1152]{2,1,0:T(4,128)(2,1)} %get-tuple-element.169), channel_id=1, source_target_pairs={{0,1},{1,2},{2,3},{4,5},{5,6},{6,7},{8,9},{9,10},{10,11},{12,13},{... | collective-permute-start | bytes 82952 | tf_op jit(solution)/shard_map/ppermute | solution.py:24
  413.9 42.5 %collective-permute-start.3 = (bf16[3,4,1152]{2,1,0:T(4,128)(2,1)}, bf16[3,4,1152]{2,1,0:T(4,128)(2,1)}, u32[]{:S(2)}, u32[]{:S(2)}) collective-permute-start(bf16[3,4,1152]{2,1,0:T(4,128)(2,1)} %get-tuple-element.170), channel_id=1, source_target_pairs={{1,0},{2,1},{3,2},{5,4},{6,5},{7,6},{9,8},{10,9},{11,10},{13,12},{... | collective-permute-start | bytes 82952 | tf_op jit(solution)/shard_map/ppermute | solution.py:27
  430.1 339.1 %all-reduce.43.cloned.1.call-start = ((), (), s32[]{:S(2)}) async-start(), calls=%async_computation.6 | async-start | bytes 35561472 | tf_op jit(solution)/shard_map/psum | solution.py:469
  (243 other events, 1148.5 us)
Sparse Core Ops, SparseCore 0:
  17.8 19.9 all-gather.4
  39.9 17.4 all-gather.2
  355.7 27.0 reduce-scatter.4
  430.2 27.0 reduce-scatter.2
  470.5 298.5 all-reduce.42
where the time goes:
time: 800 us; the launch traced here: 791 us
  waiting for transfers between devices  233 us (29%)
  matrix products  176 us (22%)
  local copies, waits for them, and re-layouts  159 us (20%)
  other arithmetic  150 us (19%)
  blocking collectives  44 us (6%)
  between operations  18 us (2%)
  starting transfers between devices  12.2 us (2%)
    psum x1, waiting for transfers between devices, shards(): lax.psum((w_project_grad, bias_query_grad, bias_value_grad, depth_kernel_...  233 us
    unnamed x563, local copies, waits for them, and re-layouts  56 us
    dot_general x1, matrix products, shards(): jnp.einsum('ngi,gio->ngo', first_low, w_inner, preferred_element_type=jnp...  44.4 us
    psum x1, blocking collectives, shards(): lax.psum((w_project_grad, bias_query_grad, bias_value_grad, depth_kernel_...  44 us
    dot_general x7, matrix products, dense_back(): lax.dot_general(left_side, right_side, (((1,), (1,)), ((), ())), preferre...  24.8 us
    dot_general x7, matrix products, dense_rows(): lax.dot_general(left_side, right_side, (((0,), (0,)), ((), ())), preferre...  18.7 us
    dot_general x8, matrix products, dense(): return jnp.dot(left_side, right_side, preferred_element_type=jnp.float32)  16.3 us
  transfers between devices with their start and end apart: 9, of which 1 were waited for; matrix products, arithmetic and copies ran while one was open for 29% of the time, Pallas kernels for 0%

commit v1 on v0

v1 whole, which is shorter than its diff:
```python
import functools

import jax
import jax.numpy as jnp
import numpy as np
from jax import lax
from jax.experimental import pallas as pl
from jax.experimental.pallas import tpu as pltpu
from jax.sharding import PartitionSpec as P

D = 768
FF = 3072
HEADS = 6
HEAD = 64
KERNEL = 9
GROUPS = 2
ALL = 384
PAIRS = 3
TAPS = HEADS * KERNEL
HALF = KERNEL // 2

F32 = jnp.float32
BF = jnp.bfloat16
ROOT_HALF = 0.7071067811865476
DENSITY = 0.3989422804014327
VMEM_BYTES = 58 * 1024 * 1024


def nn(a, b):
    return lax.dot_general(a, b, (((1,), (0,)), ((), ())), preferred_element_type=F32)


def nt(a, b):
    return lax.dot_general(a, b, (((1,), (1,)), ((), ())), preferred_element_type=F32)


def tn(a, b):
    return lax.dot_general(a, b, (((0,), (0,)), ((), ())), preferred_element_type=F32)


def tap_tables():
    perm = np.zeros((128, 128), np.float32)
    spread = np.zeros((256, PAIRS * KERNEL * 128), np.float32)
    for h in range(HEADS):
        for j in range(KERNEL):
            lane = j * HEADS + h
            perm[h * KERNEL + j, lane] = 1
            perm[h * KERNEL + j, TAPS + lane] = 1
            start = ((h // 2) * KERNEL + j) * 128 + (h % 2) * HEAD
            spread[lane, start : start + HEAD] = 1
            spread[128 + lane, start : start + HEAD] = 1
    return perm.astype(jnp.bfloat16), spread.astype(jnp.bfloat16)


def window(values, op):
    left = lambda v, n: pltpu.roll(v, 128 - n, 1)
    one = op(values, left(values, 6))
    two = op(one, left(one, 12))
    four = op(two, left(two, 24))
    return op(four, left(values, 48))


def window_sum(values):
    return window(values + pltpu.roll(values, TAPS, 1), jnp.add)


def head_stack(rows, low_half):
    zero = jnp.zeros_like(rows)
    return jnp.concatenate(
        [jnp.where(low_half, rows, zero), jnp.where(low_half, zero, rows)], axis=0
    )


def two_parts(values):
    high = values.astype(BF)
    rest = (values - high.astype(F32)).astype(BF)
    return jnp.concatenate([high, rest], axis=1)


def fill_ends(xp, x_refs, rows, sides):
    if sides is None:
        zero = jnp.zeros((8, D), F32)
        xp[0:8, :] = zero
        xp[8 + rows : 16 + rows, :] = zero
    else:
        lower, upper = sides
        xp[0:8, :] = x_refs[1][0, rows - 16 :, :].astype(F32)[8:] * lower
        xp[8 + rows : 16 + rows, :] = x_refs[-1][0, :16, :].astype(F32)[:8] * upper
    xp[8 : 8 + rows, :] = x_refs[0][0].astype(F32)


def row_sides():
    place = lax.axis_index("blk")
    count = lax.axis_size("blk")
    return (place > 0).astype(F32), (place < count - 1).astype(F32)


def pre_body(n_x, *refs):
    x_refs = refs[:n_x]
    vec, w_project, w_point, w_span, w_unfold, spread, perm = refs[n_x : n_x + 7]
    q_out, k_out, v_out, p_out, kc_out, ker_out, dl_out, up_out, mix_out = refs[n_x + 7 : n_x + 16]
    (xp,) = refs[n_x + 16 :]
    rows = x_refs[0].shape[1]
    is_long = n_x > 1
    sides = row_sides() if is_long else None
    x = x_refs[0][0]
    fill_ends(xp, x_refs, rows, sides)
    bias_query = vec[0:1, :ALL]
    bias_value = vec[0:1, ALL:]
    if is_long:
        q = (nn(x, w_project[:, :ALL]) + bias_query).astype(BF)
        for i in range(n_x):
            both = nn(x_refs[i][0], w_project[:, ALL:])
            k_out[0, i * rows : (i + 1) * rows, :] = both[:, :ALL].astype(BF)
            v_out[0, i * rows : (i + 1) * rows, :] = (both[:, ALL:] + bias_value).astype(BF)
    else:
        both = nn(x, w_project[...])
        q = (both[:, :ALL] + bias_query).astype(BF)
        k_out[0] = both[:, ALL : 2 * ALL].astype(BF)
        v_out[0] = (both[:, 2 * ALL :] + bias_value).astype(BF)
    q_out[0] = q

    for c in range(D // 128):
        cols = slice(c * 128, (c + 1) * 128)
        total = vec[12:13, cols] * xp[4 : 4 + rows, cols]
        for j in range(1, KERNEL):
            total += vec[12 + j : 13 + j, cols] * xp[4 + j : 4 + j + rows, cols]
        dl_out[0, :, cols] = total.astype(BF)
    key_conv = nn(dl_out[0], w_point[...]) + vec[1:2, :ALL]
    kc_out[0] = key_conv
    span = (key_conv * q.astype(F32)).astype(BF)
    span_weights = nn(w_span[...], perm[:TAPS, :]).astype(BF)
    span_bias = nn(vec[16:24, :128].astype(BF), perm[...])[5:6]
    logits = nn(span, span_weights) + span_bias
    lane = lax.broadcasted_iota(jnp.int32, (rows, 128), 1)
    raised = jnp.where(lane < TAPS, jnp.exp(logits - window(logits, jnp.maximum)), 0.0)
    kernel = jnp.where(lane < TAPS, raised / window_sum(raised), 0.0)
    ker_out[0] = kernel

    bias_unfold = vec[1:2, ALL:]
    up_out[0, 8 : 8 + rows, :] = nn(x, w_unfold[...]) + bias_unfold
    if is_long:
        lower, upper = sides
        ends = jnp.concatenate([x_refs[1][0, rows - 16 :, :], x_refs[-1][0, :16, :]], axis=0)
        unfold_ends = nn(ends, w_unfold[...]) + bias_unfold
        up_out[0, 0:8, :] = unfold_ends[8:16] * lower
        up_out[0, 8 + rows : 16 + rows, :] = unfold_ends[16:24] * upper
    else:
        zero = jnp.zeros((8, ALL), F32)
        up_out[0, 0:8, :] = zero
        up_out[0, 8 + rows : 16 + rows, :] = zero

    low_half = lax.broadcasted_iota(jnp.int32, (1, 128), 1) < HEAD
    parts = two_parts(kernel)
    scaled = q * jnp.asarray(HEAD ** (-0.5), BF)
    keys = k_out.shape[1]
    for p in range(PAIRS):
        cols = slice(p * 128, (p + 1) * 128)
        wide = nn(parts, spread[:, p * KERNEL * 128 : (p + 1) * KERNEL * 128])
        total = wide[:, :128] * up_out[0, 4 : 4 + rows, cols]
        for j in range(1, KERNEL):
            total += wide[:, j * 128 : (j + 1) * 128] * up_out[0, 4 + j : 4 + j + rows, cols]
        mix_out[0, :, ALL + p * 128 : ALL + (p + 1) * 128] = total.astype(BF)

        scores = nt(head_stack(k_out[0, :, cols], low_half), scaled[:, cols])
        for half in range(2):
            part = scores[half * keys : (half + 1) * keys]
            top = jnp.max(part, axis=0, keepdims=True)
            grown = jnp.exp(part - top)
            share = 1.0 / jnp.sum(grown, axis=0, keepdims=True)
            p_out[0, p, half * keys : (half + 1) * keys, :] = (grown * share).astype(BF)
        context = tn(head_stack(v_out[0, :, cols], low_half), p_out[0, p])
        mix_out[0, :, cols] = context.astype(BF).T


def block_spec(shape, index_map):
    return pl.BlockSpec(shape, index_map)


def fixed(array):
    zeros = (0,) * array.ndim
    return pl.BlockSpec(array.shape, lambda *_: zeros, pipeline_mode=pl.Buffered(1))


def per_row(*shape):
    zeros = (0,) * len(shape)
    return pl.BlockSpec((1, *shape), lambda i: (i, *zeros))


def params(**more):
    return pltpu.CompilerParams(vmem_limit_bytes=VMEM_BYTES, **more)


def pre_call(xs, consts):
    count, rows = xs[0].shape[0], xs[0].shape[1]
    keys = rows * len(xs)
    shapes = [
        ((rows, ALL), BF),
        ((keys, ALL), BF),
        ((keys, ALL), BF),
        ((PAIRS, 2 * keys, rows), BF),
        ((rows, ALL), F32),
        ((rows, 128), F32),
        ((rows, D), BF),
        ((rows + 16, ALL), F32),
        ((rows, D), BF),
    ]
    return pl.pallas_call(
        functools.partial(pre_body, len(xs)),
        grid=(count,),
        in_specs=[per_row(rows, D)] * len(xs) + [fixed(c) for c in consts],
        out_specs=[per_row(*s) for s, _ in shapes],
        out_shape=[jax.ShapeDtypeStruct((count, *s), t) for s, t in shapes],
        scratch_shapes=[pltpu.VMEM((rows + 16, D), F32)],
        compiler_params=params(),
        cost_estimate=pl.CostEstimate(
            flops=count * rows * 6_000_000, bytes_accessed=20_000_000, transcendentals=1_000_000
        ),
        name="pre_long" if len(xs) > 1 else "pre_short",
    )(*xs, *consts)


def norm_stats(z):
    centre = z - jnp.mean(z, axis=-1, keepdims=True)
    inverse = lax.rsqrt(jnp.mean(centre * centre, axis=-1, keepdims=True) + 1e-12)
    return centre * inverse, inverse


def norm_back(upstream, normed, inverse, gain):
    scaled = upstream * gain
    plain = jnp.mean(scaled, axis=-1, keepdims=True)
    cross = jnp.mean(scaled * normed, axis=-1, keepdims=True)
    return inverse * (scaled - plain - normed * cross)


def fold8(values):
    return jnp.sum(values.reshape(values.shape[0] // 8, 8, values.shape[1]), axis=0)


def gelu_pair(v):
    t = 1.0 / (1.0 + (0.3275911 * ROOT_HALF) * jnp.abs(v))
    bell = jnp.exp(-0.5 * (v * v))
    poly = 0.5 * 1.061405429
    for term in (-1.453152027, 1.421413741, -0.284496736, 0.254829592):
        poly = poly * t + 0.5 * term
    tail = poly * t * bell
    cdf = jnp.where(v >= 0, 1.0 - tail, tail)
    return v * cdf, cdf + v * bell * DENSITY


def ffn_body(masked, *refs):
    if masked:
        live_ref, *refs = refs
    (mix_ref, x_ref, cot_ref, vec, w_output, w_inner, w_outer) = refs[:7]
    (out_ref, fig_ref, mg_ref, act_ref, inl_ref, al_ref, flt_ref, olt_ref, mixt_ref, xt_ref, stat) = refs[7:18]
    (slope,) = refs[18:]
    step = pl.program_id(0)
    rows = x_ref.shape[1]

    @pl.when(step == 0)
    def _():
        stat[...] = jnp.zeros_like(stat)

    x = x_ref[0]
    mixed = mix_ref[0]
    mixt_ref[...] = mixed.T
    xt_ref[...] = x.T
    first_normed, first_inverse = norm_stats(nn(mixed, w_output[...]) + vec[2:3, :] + x.astype(F32))
    first_norm = first_normed * vec[3:4, :] + vec[4:5, :]
    first_low = first_norm.astype(BF)
    flt_ref[...] = first_low.T
    outer = []
    for g in range(GROUPS):
        for c in range(2):
            k = g * 2 + c
            inner = nn(first_low[:, g * ALL : (g + 1) * ALL], w_inner[g, :, c * D : (c + 1) * D])
            for r in range(0, rows, 16):
                act, slo = gelu_pair(inner[r : r + 16] + vec[8 + k : 9 + k, :])
                act_ref[r : r + 16, k * D : (k + 1) * D] = act.astype(BF)
                slope[r : r + 16, k * D : (k + 1) * D] = slo
        outer.append(nn(act_ref[:, g * 2 * D : (g + 1) * 2 * D], w_outer[g]))
    second_normed, second_inverse = norm_stats(
        jnp.concatenate(outer, axis=1) + vec[5:6, :] + first_norm
    )
    gain_second = vec[6:7, :]
    out_ref[0] = (second_normed * gain_second + vec[7:8, :]).astype(BF)
    seed = cot_ref[0].astype(F32)
    if masked:
        seed = jnp.where(step < live_ref[0, 0], seed, 0.0)
    stat[0:8, :] += fold8(seed * second_normed)
    stat[8:16, :] += fold8(seed)
    second_grad = norm_back(seed, second_normed, second_inverse, gain_second)
    outer_low = second_grad.astype(BF)
    olt_ref[...] = outer_low.T
    stat[32:40, :] += fold8(outer_low.astype(F32))
    first_grad = []
    for g in range(GROUPS):
        for c in range(2):
            k = g * 2 + c
            back = nt(outer_low[:, g * ALL : (g + 1) * ALL], w_outer[g, c * D : (c + 1) * D, :])
            inl_ref[:, k * D : (k + 1) * D] = (back * slope[:, k * D : (k + 1) * D]).astype(BF)
        first_grad.append(nt(inl_ref[:, g * 2 * D : (g + 1) * 2 * D], w_inner[g]))
    first_grad = second_grad + jnp.concatenate(first_grad, axis=1)
    stat[16:24, :] += fold8(first_grad * first_normed)
    stat[24:32, :] += fold8(first_grad)
    first_in_grad = norm_back(first_grad, first_normed, first_inverse, vec[3:4, :])
    fig_ref[0] = first_in_grad
    attended_low = first_in_grad.astype(BF)
    al_ref[...] = attended_low
    mg_ref[0] = nt(attended_low, w_output[...]).astype(BF)


def ffn_call(live, mixed, x, cotan, consts):
    count, rows = x.shape[0], x.shape[1]
    total = count * rows
    out_shapes = [
        ((count, rows, D), BF, per_row(rows, D)),
        ((count, rows, D), F32, per_row(rows, D)),
        ((count, rows, D), BF, per_row(rows, D)),
        ((total, FF), BF, pl.BlockSpec((rows, FF), lambda i: (i, 0))),
        ((total, FF), BF, pl.BlockSpec((rows, FF), lambda i: (i, 0))),
        ((total, D), BF, pl.BlockSpec((rows, D), lambda i: (i, 0))),
        ((D, total), BF, pl.BlockSpec((D, rows), lambda i: (0, i))),
        ((D, total), BF, pl.BlockSpec((D, rows), lambda i: (0, i))),
        ((D, total), BF, pl.BlockSpec((D, rows), lambda i: (0, i))),
        ((D, total), BF, pl.BlockSpec((D, rows), lambda i: (0, i))),
        ((40, D), F32, pl.BlockSpec((40, D), lambda i: (0, 0))),
    ]
    masked = live is not None
    head = [live] if masked else []
    head_specs = [pl.BlockSpec(memory_space=pltpu.SMEM)] if masked else []
    return pl.pallas_call(
        functools.partial(ffn_body, masked),
        grid=(count,),
        in_specs=head_specs + [per_row(rows, D)] * 3 + [fixed(c) for c in consts],
        out_specs=[s for _, _, s in out_shapes],
        out_shape=[jax.ShapeDtypeStruct(s, t) for s, t, _ in out_shapes],
        scratch_shapes=[pltpu.VMEM((rows, FF), F32)],
        compiler_params=params(),
        cost_estimate=pl.CostEstimate(
            flops=total * 12_000_000, bytes_accessed=30_000_000, transcendentals=total * FF
        ),
        name="ffn_short" if masked else "ffn_long",
    )(*head, mixed, x, cotan, *consts)


def post_body(n_x, *refs):
    is_long = n_x > 1
    x_refs = refs[:n_x]
    refs = refs[n_x:]
    (mg_ref, fig_ref, q_ref, k_ref, v_ref, p_ref, kc_ref, ker_ref, dl_ref, up_ref) = refs[:10]
    (vec, w_point, w_span, spread, perm) = refs[10:15]
    refs = refs[15:]
    if not is_long:
        (w_project, w_unfold), refs = refs[:2], refs[2:]
    (pl_out, ll_out, dlt_out, spt_out, dkg), refs = refs[:5], refs[5:]
    if is_long:
        own_out, *far_outs = refs[:n_x]
        qt_out, ug_out, tg_out = refs[n_x : n_x + 3]
        xp, dgp, prp, dq_scr = refs[n_x + 3 :]
    else:
        tg_out, ru_out, dgp, prp, dq_scr = refs
    step = pl.program_id(0)
    rows = x_refs[0].shape[1]
    keys = k_ref.shape[1]
    ext = 8 if is_long else 0

    @pl.when(step == 0)
    def _():
        dkg[...] = jnp.zeros_like(dkg)
        dgp[...] = jnp.zeros_like(dgp)
        prp[...] = jnp.zeros_like(prp)

    if is_long:
        lower, upper = row_sides()
        fill_ends(xp, x_refs, rows, (lower, upper))

    q = q_ref[0]
    qf = q.astype(F32)
    scaled = q * jnp.asarray(HEAD ** (-0.5), BF)
    low_half = lax.broadcasted_iota(jnp.int32, (1, 128), 1) < HEAD
    for p in range(PAIRS):
        cols = slice(p * 128, (p + 1) * 128)
        grad = mg_ref[0, :, cols]
        weight_grad = nt(head_stack(v_ref[0, :, cols], low_half), grad)
        low = []
        for half in range(2):
            part = slice(half * keys, (half + 1) * keys)
            probs = p_ref[0, p, part, :].astype(F32)
            inner = jnp.sum(probs * weight_grad[part], axis=0, keepdims=True)
            low.append((probs * (weight_grad[part] - inner)).astype(BF))
        score_low = jnp.concatenate(low, axis=0)
        value_grad = nn(p_ref[0, p], grad)
        value_grad = jnp.where(low_half, value_grad[:keys], value_grad[keys:])
        key_grad = nn(score_low, scaled[:, cols])
        key_grad = jnp.where(low_half, key_grad[:keys], key_grad[keys:])
        query_grad = tn(head_stack(k_ref[0, :, cols], low_half), score_low) * HEAD ** (-0.5)
        dq_scr[:, cols] = query_grad.T
        if is_long:
            own_out[0, :, cols] = key_grad[:rows]
            own_out[0, :, ALL + p * 128 : ALL + (p + 1) * 128] = value_grad[:rows]
            for i in range(1, n_x):
                block = slice(i * rows, (i + 1) * rows)
                far_outs[i - 1][0, :rows, cols] = key_grad[block].astype(BF)
                far_outs[i - 1][0, :rows, ALL + p * 128 : ALL + (p + 1) * 128] = value_grad[
                    block
                ].astype(BF)
        else:
            ru_out[:, 2 * ALL + p * 128 : 2 * ALL + (p + 1) * 128] = key_grad.astype(BF)
            ru_out[:, 3 * ALL + p * 128 : 3 * ALL + (p + 1) * 128] = value_grad.astype(BF)

    kernel = ker_ref[0]
    parts = two_parts(kernel)
    kernel_grad = jnp.zeros((rows, 128), F32)
    span_rows = rows + 2 * ext
    for p in range(PAIRS):
        cols = slice(p * 128, (p + 1) * 128)
        table = slice(p * KERNEL * 128, (p + 1) * KERNEL * 128)
        grad = mg_ref[0, :, ALL + p * 128 : ALL + (p + 1) * 128].astype(F32)
        wide = nn(parts, spread[:, table])
        products = []
        for j in range(KERNEL):
            products.append((grad * up_ref[0, 4 + j : 4 + j + rows, cols]).astype(BF))
            prp[j, 16 : 16 + rows, :] = wide[:, j * 128 : (j + 1) * 128] * grad
        kernel_grad += nt(jnp.concatenate(products, axis=1), spread[:128, table])
        first = 20 - ext
        total = prp[0, first : first + span_rows, :]
        for j in range(1, KERNEL):
            total += prp[j, first - j : first - j + span_rows, :]
        if is_long:
            ug_out[0, :, cols] = total[ext : ext + rows]
            far_outs[0][0, rows + 8 : rows + 16, cols] = (total[:ext] * lower).astype(BF)
            far_outs[-1][0, rows + 8 : rows + 16, cols] = (total[ext + rows :] * upper).astype(BF)
        else:
            ru_out[:, cols] = total.astype(BF)
    if is_long:
        zero = jnp.zeros((8, ALL), BF)
        far_outs[0][0, rows + 8 : rows + 16, ALL:] = zero
        far_outs[-1][0, rows + 8 : rows + 16, ALL:] = zero

    logit_low = (kernel * (kernel_grad - window_sum(kernel * kernel_grad))).astype(BF)
    ll_out[...] = nt(logit_low, perm[...]).astype(BF)
    span_weights = nn(w_span[...], perm[:TAPS, :]).astype(BF)
    span_grad = nt(logit_low, span_weights)
    key_conv = kc_ref[0]
    spt_out[...] = (key_conv * qf).astype(BF).T
    dlt_out[...] = dl_ref[0].T
    point_low = (span_grad * qf).astype(BF)
    pl_out[...] = point_low
    query_total = (dq_scr[...] + span_grad * key_conv).astype(BF)
    dgp[16 : 16 + rows, :] = nt(point_low, w_point[...])

    if not is_long:
        ru_out[:, ALL : 2 * ALL] = query_total
        base = nt(ru_out[:, :ALL], w_unfold[...]) + nt(ru_out[:, ALL:], w_project[...])
    else:
        qt_out[0] = query_total
    for c in range(D // 128):
        cols = slice(c * 128, (c + 1) * 128)
        x_part = xp[:, cols] if is_long else x_refs[0][0, :, cols].astype(F32)
        first = 20 - ext
        total = None
        for j in range(KERNEL):
            moved = dgp[first - j : first - j + span_rows, cols]
            term = vec[12 + j : 13 + j, cols] * moved
            total = term if total is None else total + term
            dkg[j * 8 : (j + 1) * 8, cols] += fold8(moved * x_part)
        if is_long:
            tg_out[0, :, cols] = total[ext : ext + rows] + fig_ref[0, :, cols]
            far_outs[0][0, rows : rows + 8, cols] = (total[:ext] * lower).astype(BF)
            far_outs[-1][0, rows : rows + 8, cols] = (total[ext + rows :] * upper).astype(BF)
        else:
            tg_out[0, :, cols] = total + fig_ref[0, :, cols] + base[:, cols]


def post_call(xs, mg, fig, kept, consts):
    count, rows = xs[0].shape[0], xs[0].shape[1]
    keys = rows * len(xs)
    total = count * rows
    is_long = len(xs) > 1
    q, k, v, probs, kc, ker, dl, up = kept
    row_args = [mg, fig, q, k, v, probs, kc, ker, dl, up]
    outs = [
        ((total, ALL), BF, pl.BlockSpec((rows, ALL), lambda i: (i, 0))),
        ((total, 128), BF, pl.BlockSpec((rows, 128), lambda i: (i, 0))),
        ((D, total), BF, pl.BlockSpec((D, rows), lambda i: (0, i))),
        ((ALL, total), BF, pl.BlockSpec((ALL, rows), lambda i: (0, i))),
        ((KERNEL * 8, D), F32, pl.BlockSpec((KERNEL * 8, D), lambda i: (0, 0))),
    ]
    row_out = lambda r, c, t: ((count, r, c), t, per_row(r, c))
    scratch = []
    if is_long:
        outs.append(row_out(rows, D, F32))
        for i in range(1, len(xs)):
            outs.append(row_out(rows + 16 if i in (1, len(xs) - 1) else rows, D, BF))
        outs += [row_out(rows, ALL, BF), row_out(rows, ALL, F32), row_out(rows, D, F32)]
        scratch.append(pltpu.VMEM((rows + 16, D), F32))
    else:
        outs += [
            row_out(rows, D, F32),
            ((total, 4 * ALL), BF, pl.BlockSpec((rows, 4 * ALL), lambda i: (i, 0))),
        ]
    scratch += [
        pltpu.VMEM((rows + 32, D), F32),
        pltpu.VMEM((KERNEL, rows + 32, 128), F32),
        pltpu.VMEM((rows, ALL), F32),
    ]
    return pl.pallas_call(
        functools.partial(post_body, len(xs)),
        grid=(count,),
        in_specs=[per_row(rows, D)] * len(xs)
        + [per_row(*a.shape[1:]) for a in row_args]
        + [fixed(c) for c in consts],
        out_specs=[s for _, _, s in outs],
        out_shape=[jax.ShapeDtypeStruct(s, t) for s, t, _ in outs],
        scratch_shapes=scratch,
        compiler_params=params(),
        cost_estimate=pl.CostEstimate(
            flops=total * 10_000_000, bytes_accessed=30_000_000, transcendentals=0
        ),
        name="post_long" if is_long else "post_short",
    )(*xs, *row_args, *consts)


def end_body(n_x, *refs):
    own, *rest = refs[:n_x]
    qt, ug, tg, w_project, w_unfold, out_ref, ru_out = refs[n_x:]
    rows = own.shape[1]
    both = own[0]
    for far in rest:
        both = both + far[0, :rows, :].astype(F32)
    from_next, from_prev = rest[0], rest[-1]
    unfold = ug[0]
    after = from_next[0, rows:, :].astype(F32)
    before = from_prev[0, rows:, :].astype(F32)
    middle = unfold[8 : rows - 8]
    ru_out[:, :ALL] = jnp.concatenate(
        [unfold[:8] + before[8:, :ALL], middle, unfold[rows - 8 :] + after[8:, :ALL]], axis=0
    ).astype(BF)
    ru_out[:, ALL : 2 * ALL] = qt[0]
    ru_out[:, 2 * ALL :] = both.astype(BF)
    total = nt(ru_out[:, :ALL], w_unfold[...]) + nt(ru_out[:, ALL:], w_project[...]) + tg[0]
    out_ref[0] = total
    out_ref[0, :8, :] = total[:8] + before[:8]
    out_ref[0, rows - 8 :, :] = total[rows - 8 :] + after[:8]


def end_call(own, far, qt, ug, tg, w_project, w_unfold):
    count, rows = own.shape[0], own.shape[1]
    row_args = [own, *far, qt, ug, tg]
    return pl.pallas_call(
        functools.partial(end_body, 1 + len(far)),
        grid=(count,),
        in_specs=[per_row(*a.shape[1:]) for a in row_args] + [fixed(w_project), fixed(w_unfold)],
        out_specs=[per_row(rows, D), pl.BlockSpec((rows, 4 * ALL), lambda i: (i, 0))],
        out_shape=[
            jax.ShapeDtypeStruct((count, rows, D), F32),
            jax.ShapeDtypeStruct((count * rows, 4 * ALL), BF),
        ],
        compiler_params=params(),
        cost_estimate=pl.CostEstimate(
            flops=count * rows * 2_400_000, bytes_accessed=10_000_000, transcendentals=0
        ),
        name="end_long",
    )(*row_args, w_project, w_unfold)


def grad_body(flip, sums, *refs):
    left_long, left_short, right_long, right_short, out = refs[:5]
    value = nn(left_long[...], right_long[...]) + nn(left_short[...], right_short[...])
    out[0] = value.astype(BF).T if flip else value.astype(BF)
    if sums:
        one = lambda r: jnp.ones((16, r.shape[0]), BF)
        refs[5][...] = nn(one(right_long), right_long[...]) + nn(one(right_short), right_short[...])


def grad_call(left, right, tile, groups, flip, sums, name):
    high = left[0].shape[0] // groups
    wide = right[0].shape[1] // groups
    tiles = wide // tile
    n_long, n_short = right[0].shape[0], right[1].shape[0]
    if flip:
        out_shape = [jax.ShapeDtypeStruct((groups, wide, high), BF)]
        out_specs = [pl.BlockSpec((1, tile, high), lambda g, t: (g, t, 0))]
    else:
        out_shape = [jax.ShapeDtypeStruct((groups, high, wide), BF)]
        out_specs = [pl.BlockSpec((1, high, tile), lambda g, t: (g, 0, t))]
    if sums:
        out_shape.append(jax.ShapeDtypeStruct((16, groups * wide), F32))
        out_specs.append(pl.BlockSpec((16, tile), lambda g, t: (0, g * tiles + t)))
    return pl.pallas_call(
        functools.partial(grad_body, flip, sums),
        grid=(groups, tiles),
        in_specs=[
            pl.BlockSpec((high, n_long), lambda g, t: (g, 0)),
            pl.BlockSpec((high, n_short), lambda g, t: (g, 0)),
            pl.BlockSpec((n_long, tile), lambda g, t: (0, g * tiles + t)),
            pl.BlockSpec((n_short, tile), lambda g, t: (0, g * tiles + t)),
        ],
        out_specs=out_specs,
        out_shape=out_shape,
        compiler_params=params(),
        cost_estimate=pl.CostEstimate(
            flops=2 * groups * high * wide * (n_long + n_short),
            bytes_accessed=4_000_000,
            transcendentals=0,
        ),
        name=name,
    )(*left, *right)


def shards(
    long_input,
    short_input,
    long_cotan,
    short_cotan,
    live_slots,
    w_project,
    bias_query,
    bias_value,
    depth_kernel,
    w_point,
    bias_point,
    w_span,
    bias_span,
    w_unfold,
    bias_unfold,
    w_output,
    bias_output,
    gain_first,
    shift_first,
    w_inner,
    bias_inner,
    w_outer,
    bias_outer,
    gain_second,
    shift_second,
):
    n_blk = lax.axis_size("blk")
    short_x = short_input.reshape(short_input.shape[2:])
    short_cot = short_cotan.reshape(short_cotan.shape[2:])
    vec = jnp.concatenate(
        [
            bias_query,
            bias_value,
            bias_point,
            bias_unfold,
            bias_output,
            gain_first,
            shift_first,
            bias_outer,
            gain_second,
            shift_second,
            bias_inner,
            depth_kernel.reshape(-1),
            bias_span,
            jnp.zeros((24 * D - 21 * D - TAPS,), BF),
        ]
    ).reshape(24, D).astype(F32)
    perm, spread = (jnp.asarray(t) for t in tap_tables())
    xs = [long_input] + [
        lax.ppermute(long_input, "blk", [(i, (i + k) % n_blk) for i in range(n_blk)])
        for k in range(1, n_blk)
    ]
    pre_consts = (vec, w_project, w_point, w_span, w_unfold, spread, perm)
    ffn_consts = (vec, w_output, w_inner, w_outer)
    *short_kept, short_mixed = pre_call([short_x], pre_consts)
    *long_kept, long_mixed = pre_call(xs, pre_consts)

    f_long = ffn_call(None, long_mixed, long_input, long_cotan, ffn_consts)
    f_short = ffn_call(live_slots, short_mixed, short_x, short_cot, ffn_consts)
    (l_out, l_fig, l_mg, l_act, l_inl, l_al, l_flt, l_olt, l_mixt, l_xt, l_stat) = f_long
    (s_out, s_fig, s_mg, s_act, s_inl, s_al, s_flt, s_olt, s_mixt, s_xt, s_stat) = f_short

    post_consts = (vec, w_point, w_span, spread, perm)
    l_post = post_call(xs, l_mg, l_fig, long_kept, post_consts)
    (l_pl, l_ll, l_dlt, l_spt, l_dkg), l_rest = l_post[:5], l_post[5:]
    own, far, (l_qt, l_ug, l_tg) = l_rest[0], l_rest[1:n_blk], l_rest[n_blk:]
    far = [
        lax.ppermute(a, "blk", [(i, (i - k) % n_blk) for i in range(n_blk)])
        for k, a in enumerate(far, 1)
    ]
    s_post = post_call([short_x], s_mg, s_fig, short_kept, post_consts + (w_project, w_unfold))
    s_pl, s_ll, s_dlt, s_spt, s_dkg, short_grad, s_ru = s_post
    w_inner_grad, inner_sums = grad_call((l_flt, s_flt), (l_inl, s_inl), 512, 2, False, True, "grad_inner")
    (w_outer_grad,) = grad_call((l_olt, s_olt), (l_act, s_act), 512, 2, True, False, "grad_outer")
    w_output_grad, output_sums = grad_call((l_mixt, s_mixt), (l_al, s_al), 256, 1, False, True, "grad_output")
    w_point_grad, point_sums = grad_call((l_dlt, s_dlt), (l_pl, s_pl), 128, 1, False, True, "grad_point")
    w_span_grad, span_sums = grad_call((l_spt, s_spt), (l_ll, s_ll), 128, 1, False, True, "grad_span")
    long_grad, l_ru = end_call(own, far, l_qt, l_ug, l_tg, w_project, w_unfold)
    ru_grad, ru_sums = grad_call((l_xt, s_xt), (l_ru, s_ru), 256, 1, False, True, "grad_rows")

    stat = (l_stat + s_stat).reshape(5, 8, D).sum(1)
    dkg = (l_dkg + s_dkg).reshape(KERNEL, 8, D).sum(1)
    small = jnp.concatenate(
        [
            stat.reshape(-1),
            dkg.reshape(-1),
            inner_sums[0],
            output_sums[0],
            point_sums[0],
            span_sums[0],
            ru_sums[0],
        ]
    )
    axes = ("dp", "blk")
    small = lax.psum(small, axes)
    big = lax.psum((w_inner_grad, w_outer_grad, w_output_grad, w_point_grad, w_span_grad, ru_grad), axes)
    w_inner_grad, w_outer_grad, w_output_grad, w_point_grad, w_span_grad, ru_grad = (
        b.astype(F32) for b in big
    )
    sizes = [D] * 5 + [KERNEL * D, FF, D, ALL, 128, ALL, ALL, ALL, ALL]
    places = np.cumsum([0] + sizes)
    (gs, ss, gf, sf, bo, dk, bi, bout, bp, bs, bu, bq, _, bv) = (
        small[a:b] for a, b in zip(places[:-1], places[1:])
    )
    return (
        l_out,
        s_out.reshape(short_input.shape),
        long_grad,
        short_grad.reshape(short_input.shape),
        ru_grad[0][:, ALL:],
        bq,
        bv,
        dk.reshape(KERNEL, D),
        w_point_grad[0],
        bp,
        w_span_grad[0][:, :TAPS],
        bs[:TAPS],
        ru_grad[0][:, :ALL],
        bu,
        w_output_grad[0],
        bout,
        gf,
        sf,
        w_inner_grad,
        bi,
        w_outer_grad,
        bo,
        gs,
        ss,
    )


def solution(mesh):
    rows = P("dp", "blk", None)
    slots = P("dp", "blk", None, None, None)
    in_specs = (rows, slots, rows, slots, P("dp", "blk")) + (P(),) * 20
    out_specs = (rows, slots, rows, slots) + (P(),) * 20
    return jax.shard_map(shards, mesh=mesh, in_specs=in_specs, out_specs=out_specs, check_vma=False)
```

time: 800 us -> 573 us (0.72)
  Pallas kernels: 0 us -> 208 us
  matrix products: 176 us -> 0 us
  other arithmetic: 150 us -> 8.11 us
  local copies, waits for them, and re-layouts: 159 us -> 31.5 us
  waiting for transfers between devices: 233 us -> 302 us
  blocking collectives: 44 us -> 0 us
    pallas_call x0 -> x13, Pallas kernels: none -> 208 us  [the longest x2 64.2 us: ffn_call(): pl.pallas_call(functools.partial(ffn_body, masked), grid=(count,), in_spe...]
    dot_general x39 -> x0, matrix products: 171 us -> none  [the longest x1 44.4 us: shards(): jnp.einsum('ngi,gio->ngo', first_low, w_inner, preferred_element_type=jnp...]
    psum x1 -> x2, waiting for transfers between devices: 233 us -> 301 us  [the longest x1 190 us: shards(): lax.psum((w_inner_grad, w_outer_grad, w_output_grad, w_point_grad, w_span...]
    unnamed x563 -> x42, local copies, waits for them, and re-layouts: 56 us -> 7.52 us
    reduce_sum x21 -> x2, other arithmetic: 44.3 us -> 0.12 us  [the longest x1 0.07 us: shards(): dkg = (l_dkg + s_dkg).reshape(KERNEL, 8, D).sum(1)]
    psum x1 -> x0, blocking collectives: 44 us -> none  [shards(): lax.psum((w_project_grad, bias_query_grad, bias_value_grad, depth_kernel_...]
    convert_element_type x28 -> x2, other arithmetic: 45.7 us -> 5.31 us  [shards(): b.astype(F32)]
    mul x5 -> x0, other arithmetic: 28.3 us -> none  [the longest x1 15.6 us: conv_back(): kernel[:, :, :, offset, None] * grad_heads]
  transfers between devices with their start and end apart: 9 -> 8, of which waited for: 1 -> 3; matrix products, arithmetic and copies ran while one was open for 29% -> 4% of each run, Pallas kernels for 0% -> 24%
where the time goes in v1:
time: 573 us; the launch traced here: 571 us
  waiting for transfers between devices  302 us (53%)
  Pallas kernels  208 us (36%)
  local copies, waits for them, and re-layouts  31.5 us (5%)
  between operations  14.9 us (3%)
  other arithmetic  8.11 us (1%)
  starting transfers between devices  6.37 us (1%)
    psum x1, waiting for transfers between devices, shards(): lax.psum((w_inner_grad, w_outer_grad, w_output_grad, w_point_grad, w_span...  190 us
    psum x1, waiting for transfers between devices, shards(): small = lax.psum(small, axes)  110 us
    pallas_call x2, Pallas kernels, ffn_call(): pl.pallas_call(functools.partial(ffn_body, masked), grid=(count,), in_spe...  64.2 us
    pallas_call x2, Pallas kernels, post_call(): pl.pallas_call(functools.partial(post_body, len(xs)), grid=(count,), in_s...  53.4 us
    pallas_call x2, Pallas kernels, pre_call(): pl.pallas_call(functools.partial(pre_body, len(xs)), grid=(count,), in_sp...  42.6 us
    pallas_call x6, Pallas kernels, grad_call(): pl.pallas_call(functools.partial(grad_body, flip, sums), grid=(groups, ti...  40.8 us
  transfers between devices with their start and end apart: 8, of which 3 were waited for; matrix products, arithmetic and copies ran while one was open for 4% of the time, Pallas kernels for 24%

profile of v1, /device:TPU:1, one launch (start us, length us, event | category | flops | bytes accessed | tf_op | source)
XLA Modules:
  0.0 570.6 jit_solution(10125987860645174899)
XLA Ops:
  7.3 2.7 collective-permute-start.1
  12.8 8.3 %concatenate.6 = bf16[18432]{0:T(1024)(128)(2,1)S(1)} concatenate(bf16[384]{0:T(512)(128)(2,1)} %param.33, bf16[384]{0:T(512)(128)(2,1)} %param.34, bf16[384]{0:T(512)(128)(2,1)} %param.37, bf16[384]{0:T(512)(128)(2,1)} %param.41, bf16[768]{0:T(1024)(128)(2,1)} %param.43, bf16[768]{0:T(1024)(128)(2,1)} %param.44, bf16[768]{0:T(1024)(128)(2,1)} %param.45, bf16[768]{0:T(1024)(128)(2,1)} %param.49, ...), dimensions={0} | concatenate | bytes 73728 | tf_op jit(solution)/shard_map/concatenate | solution.py:642
  21.8 1.5 copy.51.refs_7_.refs_4_.refs_16_.refs_13_
  23.3 26.3 %pre_short.1 = (bf16[8,128,384]{2,1,0:T(8,128)(2,1)}, bf16[8,128,384]{2,1,0:T(8,128)(2,1)}, bf16[8,128,384]{2,1,0:T(8,128)(2,1)}, bf16[8,3,256,128]{3,2,1,0:T(8,...) custom-call(bf16[8,128,768]{2,1,0:T(8,128)(2,1)} %bitcast.21, ...), custom_call_target="tpu_custom_call" | custom-call | flops 6144000000 | bytes 20000000 | tf_op jit(solution)/shard_map/pre_short/pallas_call | solution.py:208
  49.6 44.8 %ffn_short.1 = (bf16[8,128,768]{2,1,0:T(8,128)(2,1)}, f32[8,128,768]{2,1,0:T(8,128)}, bf16[8,128,768]{2,1,0:T(8,128)(2,1)}, bf16[1024,3072]{1,0:T(8,128)(2,1)}, ...) custom-call(s32[1,1]{1,0:T(1,128)S(6)} %copy.70.refs_0_, ...), custom_call_target="tpu_custom_call" | custom-call | flops 12288000000 | bytes 30000000 | tf_op jit(solution)/shard_map/ffn_short/pallas_call | solution.py:332
  94.5 35.4 %post_short.1 = (bf16[1024,384]{1,0:T(8,128)(2,1)}, bf16[1024,128]{1,0:T(8,128)(2,1)}, bf16[768,1024]{1,0:T(8,128)(2,1)}, bf16[384,1024]{1,0:T(8,128)(2,1)}, f32...) custom-call(bf16[8,128,768]{2,1,0:T(8,128)(2,1)} %bitcast.23, ...), custom_call_target="tpu_custom_call" | custom-call | flops 10240000000 | bytes 30000000 | tf_op jit(solution)/shard_map/post_short/pallas_call | solution.py:508
  131.8 16.3 %pre_long.1 = (bf16[3,128,384]{2,1,0:T(8,128)(2,1)}, bf16[3,512,384]{2,1,0:T(8,128)(2,1)}, bf16[3,512,384]{2,1,0:T(8,128)(2,1)}, bf16[3,3,1024,128]{3,2,1,0:T(8,...) custom-call(bf16[3,128,768]{2,1,0:T(8,128)(2,1)} %refs_0_.4, ...), custom_call_target="tpu_custom_call" | custom-call | flops 2304000000 | bytes 20000000 | tf_op jit(solution)/shard_map/pre_long/pallas_call | solution.py:208
  148.0 19.4 %ffn_long.1 = (bf16[3,128,768]{2,1,0:T(8,128)(2,1)}, f32[3,128,768]{2,1,0:T(8,128)}, bf16[3,128,768]{2,1,0:T(8,128)(2,1)}, bf16[384,3072]{1,0:T(8,128)(2,1)}, bf...) custom-call(bf16[3,128,768]{2,1,0:T(8,128)(2,1)} %get-tuple-element., ...), custom_call_target="tpu_custom_call" | custom-call | flops 4608000000 | bytes 30000000 | tf_op jit(solution)/shard_map/ffn_long/pallas_call | solution.py:332
  167.4 18.1 %post_long.1 = (bf16[384,384]{1,0:T(8,128)(2,1)}, bf16[384,128]{1,0:T(8,128)(2,1)}, bf16[768,384]{1,0:T(8,128)(2,1)}, bf16[384,384]{1,0:T(8,128)(2,1)}, f32[72,7...) custom-call(bf16[3,128,768]{2,1,0:T(8,128)(2,1)} %refs_0_.4, ...), custom_call_target="tpu_custom_call" | custom-call | flops 3840000000 | bytes 30000000 | tf_op jit(solution)/shard_map/post_long/pallas_call | solution.py:508
  186.0 1.7 collective-permute-start.5
  187.7 9.4 %grad_inner.1 = (bf16[2,384,1536]{2,1,0:T(8,128)(2,1)}, f32[16,3072]{1,0:T(8,128)}) custom-call(bf16[768,384]{1,0:T(8,128)(2,1)} %get-tuple-element.137.refs_0_, bf16[768,1024]{1,0:T(8,128)(2,1)} %get-tuple-element.138.refs_1_, bf16[384,3072]{1,0:T(8,128)(2,1)} %get-tuple-element.139.refs_2_, bf16[1024,3072]{1,0:T(8,128)(2,1)} %get-tuple-element.140.refs_3_), custom_call_target="tpu_custom_call" | custom-call | flops 3321888768 | bytes 4000000 | tf_op jit(solution)/shard_map/grad_inner/pallas_call | solution.py:591
  198.1 5.7 %grad_output.1 = (bf16[1,768,768]{2,1,0:T(8,128)(2,1)}, f32[16,768]{1,0:T(8,128)}) custom-call(bf16[768,384]{1,0:T(8,128)(2,1)} %get-tuple-element.142.refs_0_, bf16[768,1024]{1,0:T(8,128)(2,1)} %get-tuple-element.143.refs_1_, bf16[384,768]{1,0:T(8,128)(2,1)} %get-tuple-element.144.refs_2_, bf16[1024,768]{1,0:T(8,128)(2,1)} %get-tuple-element.145.refs_3_), custom_call_target="tpu_custom_call" | custom-call | flops 1660944384 | bytes 4000000 | tf_op jit(solution)/shard_map/grad_output/pallas_call | solution.py:591
  204.7 5.1 grad_point.1
  209.8 2.4 grad_span.1
  215.7 6.7 %end_long.1 = (f32[3,128,768]{2,1,0:T(8,128)}, bf16[384,1536]{1,0:T(8,128)(2,1)}) custom-call(f32[3,128,768]{2,1,0:T(8,128)} %get-tuple-element.109.refs_0_, bf16[3,144,768]{2,1,0:T(8,128)(2,1)} %copy-done.4, bf16[3,128,768]{2,1,0:T(8,128)(2,1)} %copy-done.6, bf16[3,144,768]{2,1,0:T(8,128)(2,1)} %copy-done.5, ...), custom_call_target="tpu_custom_call" | custom-call | flops 921600000 | bytes 10000000 | tf_op jit(solution)/shard_map/end_long/pallas_call | solution.py:551
  222.5 8.7 %grad_rows.1 = (bf16[1,768,1536]{2,1,0:T(8,128)(2,1)}, f32[16,1536]{1,0:T(8,128)}) custom-call(bf16[768,384]{1,0:T(8,128)(2,1)} %get-tuple-element.128.refs_0_, bf16[768,1024]{1,0:T(8,128)(2,1)} %get-tuple-element.129.refs_1_, bf16[384,1536]{1,0:T(8,128)(2,1)} %get-tuple-element.130.refs_2_, bf16[1024,1536]{1,0:T(8,128)(2,1)} %get-tuple-element.131.refs_3_), custom_call_target="tpu_custom_call" | custom-call | flops 3321888768 | bytes 4000000 | tf_op jit(solution)/shard_map/grad_rows/pallas_call | solution.py:591
  232.8 9.4 %grad_outer.1 = bf16[2,1536,384]{2,1,0:T(8,128)(2,1)} custom-call(bf16[768,384]{1,0:T(8,128)(2,1)} %get-tuple-element.162.refs_0_, bf16[768,1024]{1,0:T(8,128)(2,1)} %get-tuple-element.163.refs_1_, bf16[384,3072]{1,0:T(8,128)(2,1)} %get-tuple-element.164.refs_2_, bf16[1024,3072]{1,0:T(8,128)(2,1)} %get-tuple-element.165.refs_3_), custom_call_target="tpu_custom_call" | custom-call | flops 3321888768 | bytes 4000000 | tf_op jit(solution)/shard_map/grad_outer/pallas_call | solution.py:591
  242.2 110.4 %all-reduce.4.cloned.1.call-done = f32[16640]{0:T(1024)} async-done(((f32[16640]{0:T(1024)}), f32[16640]{0:T(1024)}) %all-reduce.4.cloned.1.call-update) | async-done | bytes 66576 | tf_op jit(solution)/shard_map/psum | solution.py:707
  359.3 190.5 %all-reduce.6.cloned.1.call-done = (bf16[768,1536]{1,0:T(8,128)(2,1)}, bf16[768,384]{1,0:T(8,128)(2,1)}, bf16[384,128]{1,0:T(8,128)(2,1)}, bf16[768,768]{1,0:T(8...) async-done(((bf16[768,1536]{1,0:T(8,128)(2,1)}, bf16[768,384]{1,0:T(8,128)(2,1)}, bf16[384,128]{1,0:T(8,128)(2,1)}, bf16[768,768]{1,0:T(8,128)(2,1)}, ...) | async-done | bytes 8945680 | tf_op jit(solution)/shard_map/psum | solution.py:708
  549.7 2.3 slice.97
  552.1 2.0 slice.90
  556.0 1.6 squeeze.49
  558.5 2.8 convert_element_type.17
  561.3 2.5 convert_element_type.18
  (76 shorter events, 21.6 us)
Async XLA Ops:
  7.2 345.4 %all-reduce.4.cloned.1.call-start = ((), (), s32[]{:S(2)}) async-start(), calls=%async_computation | async-start | bytes 139264 | tf_op jit(solution)/shard_map/psum | solution.py:707
  7.2 122.6 %collective-permute-start.2 = (bf16[3,128,768]{2,1,0:T(8,128)(2,1)}, bf16[3,128,768]{2,1,0:T(8,128)(2,1)S(1)}, u32[]{:S(2)}, u32[]{:S(2)}) collective-permute-start(bf16[3,128,768]{2,1,0:T(8,128)(2,1)} %refs_0_.4), channel_id=1, source_target_pairs={{0,3},{1,0},{2,1},{3,2},{4,7},{5,4},{6,5},{7,6},{8,11},{9,8},{10,9... | collective-permute-start | bytes 1769480 | tf_op jit(solution)/shard_map/ppermute | solution.py:662
  7.3 122.5 %collective-permute-start.1 = (bf16[3,128,768]{2,1,0:T(8,128)(2,1)}, bf16[3,128,768]{2,1,0:T(8,128)(2,1)S(1)}, u32[]{:S(2)}, u32[]{:S(2)}) collective-permute-start(bf16[3,128,768]{2,1,0:T(8,128)(2,1)} %refs_0_.4), channel_id=1, source_target_pairs={{0,2},{1,3},{2,0},{3,1},{4,6},{5,7},{6,4},{7,5},{8,10},{9,11},{10,... | collective-permute-start | bytes 1769480 | tf_op jit(solution)/shard_map/ppermute | solution.py:662
  10.0 119.9 %collective-permute-start = (bf16[3,128,768]{2,1,0:T(8,128)(2,1)}, bf16[3,128,768]{2,1,0:T(8,128)(2,1)S(1)}, u32[]{:S(2)}, u32[]{:S(2)}) collective-permute-start(bf16[3,128,768]{2,1,0:T(8,128)(2,1)} %refs_0_.4), channel_id=1, source_target_pairs={{0,1},{1,2},{2,3},{3,0},{4,5},{5,6},{6,7},{7,4},{8,9},{9,10},{10,1... | collective-permute-start | bytes 1769480 | tf_op jit(solution)/shard_map/ppermute | solution.py:662
  129.9 0.8 copy-start.14
  129.9 1.0 copy-start.15
  130.9 0.8 copy-start.16
  185.5 28.2 %collective-permute-start.4 = (bf16[3,128,768]{2,1,0:T(8,128)(2,1)}, bf16[3,128,768]{2,1,0:T(8,128)(2,1)S(1)}, u32[]{:S(2)}, u32[]{:S(2)}) collective-permute-start(bf16[3,128,768]{2,1,0:T(8,128)(2,1)} %get-tuple-element.111), channel_id=1, source_target_pairs={{0,2},{1,3},{2,0},{3,1},{4,6},{5,7},{6,4},{7,5},{8,10},{9,11},{10,... | collective-permute-start | bytes 1769480 | tf_op jit(solution)/shard_map/ppermute | solution.py:680
  185.9 28.8 %collective-permute-start.3 = (bf16[3,144,768]{2,1,0:T(8,128)(2,1)}, bf16[3,144,768]{2,1,0:T(8,128)(2,1)S(1)}, u32[]{:S(2)}, u32[]{:S(2)}) collective-permute-start(bf16[3,144,768]{2,1,0:T(8,128)(2,1)} %get-tuple-element.110), channel_id=1, source_target_pairs={{0,3},{1,0},{2,1},{3,2},{4,7},{5,4},{6,5},{7,6},{8,11},{9,8},{10,9... | collective-permute-start | bytes 1990664 | tf_op jit(solution)/shard_map/ppermute | solution.py:680
  186.0 28.7 %collective-permute-start.5 = (bf16[3,144,768]{2,1,0:T(8,128)(2,1)}, bf16[3,144,768]{2,1,0:T(8,128)(2,1)S(1)}, u32[]{:S(2)}, u32[]{:S(2)}) collective-permute-start(bf16[3,144,768]{2,1,0:T(8,128)(2,1)} %get-tuple-element.112), channel_id=1, source_target_pairs={{0,1},{1,2},{2,3},{3,0},{4,5},{5,6},{6,7},{7,4},{8,9},{9,10},{10,1... | collective-permute-start | bytes 1990664 | tf_op jit(solution)/shard_map/ppermute | solution.py:680
  187.7 10.3 %copy-start.10 = (f32[40,768]{1,0:T(8,128)S(1)}, f32[40,768]{1,0:T(8,128)}, u32[]{:S(2)}) copy-start(f32[40,768]{1,0:T(8,128)} %get-tuple-element.134) | copy-start | bytes 368644
  187.7 10.3 %copy-start.11 = (f32[40,768]{1,0:T(8,128)S(1)}, f32[40,768]{1,0:T(8,128)}, u32[]{:S(2)}) copy-start(f32[40,768]{1,0:T(8,128)} %get-tuple-element.133) | copy-start | bytes 368644
  198.0 6.5 %copy-start.8 = (f32[72,768]{1,0:T(8,128)S(1)}, f32[72,768]{1,0:T(8,128)}, u32[]{:S(2)}) copy-start(f32[72,768]{1,0:T(8,128)} %get-tuple-element.136) | copy-start | bytes 663556
  198.1 6.5 %copy-start.9 = (f32[72,768]{1,0:T(8,128)S(1)}, f32[72,768]{1,0:T(8,128)}, u32[]{:S(2)}) copy-start(f32[72,768]{1,0:T(8,128)} %get-tuple-element.135) | copy-start | bytes 663556
  213.7 1.0 copy-start.6
  214.7 0.8 copy-start.4
  214.7 1.1 copy-start.5
  232.7 317.0 %all-reduce.6.cloned.1.call-start = ((), (), s32[]{:S(2)}) async-start(), calls=%async_computation.1 | async-start | bytes 17891328 | tf_op jit(solution)/shard_map/psum | solution.py:708
  549.7 2.3 copy-start
  552.0 2.0 copy-start.12
  552.1 2.8 copy-start.7
  554.1 1.9 copy-start.3
  556.0 2.5 copy-start.2
  558.5 2.8 copy-start.1
  (1 other events, 0.6 us)
Sparse Core Ops, SparseCore 0:
  232.8 119.6 all-reduce.3
  360.1 189.5 all-reduce.5

commit v2 on v1

--- a/solution.py
+++ b/solution.py
@@ -251,9 +251,11 @@
 def ffn_body(masked, *refs):
     if masked:
         live_ref, *refs = refs
+        refs = refs[:7] + refs[9:]
     (mix_ref, x_ref, cot_ref, vec, w_output, w_inner, w_outer) = refs[:7]
-    (out_ref, fig_ref, mg_ref, act_ref, inl_ref, al_ref, flt_ref, olt_ref, mixt_ref, xt_ref, stat) = refs[7:18]
-    (slope,) = refs[18:]
+    (out_ref, fig_ref, mg_ref, left, right, stat) = refs[7:13]
+    (slope,) = refs[13:]
+    inl_ref, act_ref = right.at[:, :FF], right.at[:, FF : 2 * FF]
     step = pl.program_id(0)
     rows = x_ref.shape[1]
 
@@ -263,12 +265,12 @@
 
     x = x_ref[0]
     mixed = mix_ref[0]
-    mixt_ref[...] = mixed.T
-    xt_ref[...] = x.T
+    left[2 * D : 3 * D, :] = mixed.T
+    left[3 * D :, :] = x.T
     first_normed, first_inverse = norm_stats(nn(mixed, w_output[...]) + vec[2:3, :] + x.astype(F32))
     first_norm = first_normed * vec[3:4, :] + vec[4:5, :]
     first_low = first_norm.astype(BF)
-    flt_ref[...] = first_low.T
+    left[:D, :] = first_low.T
     outer = []
     for g in range(GROUPS):
         for c in range(2):
@@ -291,7 +293,7 @@
     stat[8:16, :] += fold8(seed)
     second_grad = norm_back(seed, second_normed, second_inverse, gain_second)
     outer_low = second_grad.astype(BF)
-    olt_ref[...] = outer_low.T
+    left[D : 2 * D, :] = outer_low.T
     stat[32:40, :] += fold8(outer_low.astype(F32))
     first_grad = []
     for g in range(GROUPS):
@@ -306,42 +308,42 @@
     first_in_grad = norm_back(first_grad, first_normed, first_inverse, vec[3:4, :])
     fig_ref[0] = first_in_grad
     attended_low = first_in_grad.astype(BF)
-    al_ref[...] = attended_low
+    right[:, 2 * FF :] = attended_low
     mg_ref[0] = nt(attended_low, w_output[...]).astype(BF)
 
 
-def ffn_call(live, mixed, x, cotan, consts):
+def ffn_call(live, mixed, x, cotan, consts, joint, tokens):
     count, rows = x.shape[0], x.shape[1]
     total = count * rows
+    masked = live is not None
+    first = tokens // rows - count if masked else 0
     out_shapes = [
         ((count, rows, D), BF, per_row(rows, D)),
         ((count, rows, D), F32, per_row(rows, D)),
         ((count, rows, D), BF, per_row(rows, D)),
-        ((total, FF), BF, pl.BlockSpec((rows, FF), lambda i: (i, 0))),
-        ((total, FF), BF, pl.BlockSpec((rows, FF), lambda i: (i, 0))),
-        ((total, D), BF, pl.BlockSpec((rows, D), lambda i: (i, 0))),
-        ((D, total), BF, pl.BlockSpec((D, rows), lambda i: (0, i))),
-        ((D, total), BF, pl.BlockSpec((D, rows), lambda i: (0, i))),
-        ((D, total), BF, pl.BlockSpec((D, rows), lambda i: (0, i))),
-        ((D, total), BF, pl.BlockSpec((D, rows), lambda i: (0, i))),
+        ((4 * D, tokens), BF, pl.BlockSpec((4 * D, rows), lambda i: (0, first + i))),
+        ((tokens, 2 * FF + D), BF, pl.BlockSpec((rows, 2 * FF + D), lambda i: (first + i, 0))),
         ((40, D), F32, pl.BlockSpec((40, D), lambda i: (0, 0))),
     ]
-    masked = live is not None
     head = [live] if masked else []
     head_specs = [pl.BlockSpec(memory_space=pltpu.SMEM)] if masked else []
     return pl.pallas_call(
         functools.partial(ffn_body, masked),
         grid=(count,),
-        in_specs=head_specs + [per_row(rows, D)] * 3 + [fixed(c) for c in consts],
+        in_specs=head_specs
+        + [per_row(rows, D)] * 3
+        + [fixed(c) for c in consts]
+        + [pl.BlockSpec(memory_space=pl.ANY)] * len(joint),
         out_specs=[s for _, _, s in out_shapes],
         out_shape=[jax.ShapeDtypeStruct(s, t) for s, t, _ in out_shapes],
         scratch_shapes=[pltpu.VMEM((rows, FF), F32)],
+        input_output_aliases={8: 3, 9: 4} if masked else {},
         compiler_params=params(),
         cost_estimate=pl.CostEstimate(
             flops=total * 12_000_000, bytes_accessed=30_000_000, transcendentals=total * FF
         ),
         name="ffn_short" if masked else "ffn_long",
-    )(*head, mixed, x, cotan, *consts)
+    )(*head, mixed, x, cotan, *consts, *joint)
 
 
 def post_body(n_x, *refs):
@@ -352,8 +354,8 @@
     (vec, w_point, w_span, spread, perm) = refs[10:15]
     refs = refs[15:]
     if not is_long:
-        (w_project, w_unfold), refs = refs[:2], refs[2:]
-    (pl_out, ll_out, dlt_out, spt_out, dkg), refs = refs[:5], refs[5:]
+        (w_project, w_unfold), refs = refs[:2], refs[4:]
+    (left, right, dkg), refs = refs[:3], refs[3:]
     if is_long:
         own_out, *far_outs = refs[:n_x]
         qt_out, ug_out, tg_out = refs[n_x : n_x + 3]
@@ -439,14 +441,14 @@
         far_outs[-1][0, rows + 8 : rows + 16, ALL:] = zero
 
     logit_low = (kernel * (kernel_grad - window_sum(kernel * kernel_grad))).astype(BF)
-    ll_out[...] = nt(logit_low, perm[...]).astype(BF)
+    left[D:, :] = nt(perm[...], logit_low).astype(BF)
     span_weights = nn(w_span[...], perm[:TAPS, :]).astype(BF)
     span_grad = nt(logit_low, span_weights)
     key_conv = kc_ref[0]
-    spt_out[...] = (key_conv * qf).astype(BF).T
-    dlt_out[...] = dl_ref[0].T
+    right[:, ALL:] = (key_conv * qf).astype(BF)
+    left[:D, :] = dl_ref[0].T
     point_low = (span_grad * qf).astype(BF)
-    pl_out[...] = point_low
+    right[:, :ALL] = point_low
     query_total = (dq_scr[...] + span_grad * key_conv).astype(BF)
     dgp[16 : 16 + rows, :] = nt(point_low, w_point[...])
 
@@ -473,18 +475,16 @@
             tg_out[0, :, cols] = total + fig_ref[0, :, cols] + base[:, cols]
 
 
-def post_call(xs, mg, fig, kept, consts):
+def post_call(xs, mg, fig, kept, consts, joint, tokens):
     count, rows = xs[0].shape[0], xs[0].shape[1]
     keys = rows * len(xs)
     total = count * rows
     is_long = len(xs) > 1
-    q, k, v, probs, kc, ker, dl, up = kept
-    row_args = [mg, fig, q, k, v, probs, kc, ker, dl, up]
+    first = 0 if is_long else tokens // rows - count
+    row_args = [mg, fig, *kept]
     outs = [
-        ((total, ALL), BF, pl.BlockSpec((rows, ALL), lambda i: (i, 0))),
-        ((total, 128), BF, pl.BlockSpec((rows, 128), lambda i: (i, 0))),
-        ((D, total), BF, pl.BlockSpec((D, rows), lambda i: (0, i))),
-        ((ALL, total), BF, pl.BlockSpec((ALL, rows), lambda i: (0, i))),
+        ((D + 128, tokens), BF, pl.BlockSpec((D + 128, rows), lambda i: (0, first + i))),
+        ((tokens, 2 * ALL), BF, pl.BlockSpec((rows, 2 * ALL), lambda i: (first + i, 0))),
         ((KERNEL * 8, D), F32, pl.BlockSpec((KERNEL * 8, D), lambda i: (0, 0))),
     ]
     row_out = lambda r, c, t: ((count, r, c), t, per_row(r, c))
@@ -498,33 +498,36 @@
     else:
         outs += [
             row_out(rows, D, F32),
-            ((total, 4 * ALL), BF, pl.BlockSpec((rows, 4 * ALL), lambda i: (i, 0))),
+            ((tokens, 4 * ALL), BF, pl.BlockSpec((rows, 4 * ALL), lambda i: (first + i, 0))),
         ]
     scratch += [
         pltpu.VMEM((rows + 32, D), F32),
         pltpu.VMEM((KERNEL, rows + 32, 128), F32),
         pltpu.VMEM((rows, ALL), F32),
     ]
+    inputs = [*xs, *row_args, *consts]
     return pl.pallas_call(
         functools.partial(post_body, len(xs)),
         grid=(count,),
         in_specs=[per_row(rows, D)] * len(xs)
         + [per_row(*a.shape[1:]) for a in row_args]
-        + [fixed(c) for c in consts],
+        + [fixed(c) for c in consts]
+        + [pl.BlockSpec(memory_space=pl.ANY)] * len(joint),
         out_specs=[s for _, _, s in outs],
         out_shape=[jax.ShapeDtypeStruct(s, t) for s, t, _ in outs],
         scratch_shapes=scratch,
+        input_output_aliases={len(inputs) + i: i for i in range(len(joint))},
         compiler_params=params(),
         cost_estimate=pl.CostEstimate(
             flops=total * 10_000_000, bytes_accessed=30_000_000, transcendentals=0
         ),
         name="post_long" if is_long else "post_short",
-    )(*xs, *row_args, *consts)
+    )(*inputs, *joint)
 
 
 def end_body(n_x, *refs):
     own, *rest = refs[:n_x]
-    qt, ug, tg, w_project, w_unfold, out_ref, ru_out = refs[n_x:]
+    qt, ug, tg, w_project, w_unfold, _, out_ref, ru_out = refs[n_x:]
     rows = own.shape[1]
     both = own[0]
     for far in rest:
@@ -545,68 +548,411 @@
     out_ref[0, rows - 8 :, :] = total[rows - 8 :] + after[:8]
 
 
-def end_call(own, far, qt, ug, tg, w_project, w_unfold):
+def end_call(own, far, qt, ug, tg, w_project, w_unfold, joint):
     count, rows = own.shape[0], own.shape[1]
     row_args = [own, *far, qt, ug, tg]
     return pl.pallas_call(
         functools.partial(end_body, 1 + len(far)),
         grid=(count,),
-        in_specs=[per_row(*a.shape[1:]) for a in row_args] + [fixed(w_project), fixed(w_unfold)],
+        in_specs=[per_row(*a.shape[1:]) for a in row_args]
+        + [fixed(w_project), fixed(w_unfold), pl.BlockSpec(memory_space=pl.ANY)],
         out_specs=[per_row(rows, D), pl.BlockSpec((rows, 4 * ALL), lambda i: (i, 0))],
         out_shape=[
             jax.ShapeDtypeStruct((count, rows, D), F32),
-            jax.ShapeDtypeStruct((count * rows, 4 * ALL), BF),
+            jax.ShapeDtypeStruct(joint.shape, BF),
         ],
+        input_output_aliases={len(row_args) + 2: 1},
         compiler_params=params(),
         cost_estimate=pl.CostEstimate(
             flops=count * rows * 2_400_000, bytes_accessed=10_000_000, transcendentals=0
         ),
         name="end_long",
-    )(*row_args, w_project, w_unfold)
-
-
-def grad_body(flip, sums, *refs):
-    left_long, left_short, right_long, right_short, out = refs[:5]
-    value = nn(left_long[...], right_long[...]) + nn(left_short[...], right_short[...])
-    out[0] = value.astype(BF).T if flip else value.astype(BF)
-    if sums:
-        one = lambda r: jnp.ones((16, r.shape[0]), BF)
-        refs[5][...] = nn(one(right_long), right_long[...]) + nn(one(right_short), right_short[...])
-
-
-def grad_call(left, right, tile, groups, flip, sums, name):
-    high = left[0].shape[0] // groups
-    wide = right[0].shape[1] // groups
-    tiles = wide // tile
-    n_long, n_short = right[0].shape[0], right[1].shape[0]
-    if flip:
-        out_shape = [jax.ShapeDtypeStruct((groups, wide, high), BF)]
-        out_specs = [pl.BlockSpec((1, tile, high), lambda g, t: (g, t, 0))]
-    else:
-        out_shape = [jax.ShapeDtypeStruct((groups, high, wide), BF)]
-        out_specs = [pl.BlockSpec((1, high, tile), lambda g, t: (g, 0, t))]
-    if sums:
-        out_shape.append(jax.ShapeDtypeStruct((16, groups * wide), F32))
-        out_specs.append(pl.BlockSpec((16, tile), lambda g, t: (0, g * tiles + t)))
+    )(*row_args, w_project, w_unfold, joint)
+
+
+UNIT = 3 * ALL
+CHUNK = 4 * UNIT
+CHUNKS = 8
+LAST = 6 * 512
+PACKED = (CHUNKS - 1) * CHUNK + LAST
+SPAN_ROW = (CHUNKS - 1) * CHUNK + 2 * UNIT
+SMALL_ROW = SPAN_ROW + ALL
+SMALL = 48
+MESH = pl.DeviceIdType.MESH
+
+
+def chunk_parts(k):
+    blocks = CHUNK // 512 if k < CHUNKS - 1 else LAST // 512
+    first = (blocks + 1) // 2 if k % 2 == 0 else blocks // 2
+    start = k * CHUNK
+    middle = start + first * 512
+    return [(start, first * 512, "cxy"), (middle, (blocks - first) * 512, "cyx")]
+
+
+def rows_of(ref, start, count):
+    return ref.at[pl.ds(pl.multiple_of(start, 16), count), :]
+
+
+def add_rows(out, start, sources, count):
+    step = next(s for s in (160, 128, 96, 80, 64, 48, 32, 16) if count % s == 0)
+
+    def body(i, carry):
+        total = None
+        for ref, first in sources:
+            value = rows_of(ref, first + i * step, step)[...].astype(F32)
+            total = value if total is None else total + value
+        rows_of(out, start + i * step, step)[...] = total.astype(BF)
+        return carry
+
+    lax.fori_loop(0, count // step, body, 0)
+
+
+class Exchange:
+    def __init__(self, part, res, out, scratch):
+        self.part, self.res, self.out = part, res, out
+        self.got = scratch[0:3]
+        self.got_z = scratch[3]
+        self.acc = scratch[4:7]
+        self.send_sem, self.recv_sem, self.out_sem = scratch[7:10]
+        dp, blk = lax.axis_index("dp"), lax.axis_index("blk")
+        core, x, y, z = lax.rem(blk, 2), blk // 2, lax.rem(dp, 2), dp // 2
+        self.z = z
+        self.bit = {"c": core, "x": x, "y": y}
+        self.peer = {
+            "c": (dp, blk + 1 - 2 * core),
+            "x": (dp, blk + 2 - 4 * x),
+            "y": (dp + 1 - 2 * y, blk),
+        }
+        self.z_peer = [(lax.rem(z + i, 4) * 2 + y, blk) for i in (1, 2, 3)]
+        self.open = {}
+        self.sends = []
+        self.place = {}
+
+    def greet(self):
+        barrier = pltpu.get_barrier_semaphore()
+        for device in [*self.peer.values(), *self.z_peer]:
+            pl.semaphore_signal(barrier, inc=1, device_id=device, device_id_type=MESH)
+
+    def await_greetings(self):
+        pl.semaphore_wait(pltpu.get_barrier_semaphore(), 6)
+
+    def start(self, n, slot, source, target, device):
+        copy = pltpu.make_async_remote_copy(
+            src_ref=source,
+            dst_ref=target,
+            send_sem=self.send_sem.at[n, slot],
+            recv_sem=self.recv_sem.at[n, slot],
+            device_id=device,
+            device_id_type=MESH,
+        )
+        copy.start()
+        self.open[n, slot] = copy
+        self.sends.append(copy)
+
+    def stage(self, n, part, s):
+        row, count, order = part
+        bit, peer, acc, got, res = self.bit, self.peer, self.acc, self.got, self.res
+        if 1 <= s <= 3:
+            size = count >> s
+            self.open[n, s - 1].wait_recv()
+            before, first = (self.part, row) if s == 1 else (acc[s - 2], row >> (s - 1))
+            mine = first + bit[order[s - 1]] * size
+            add_rows(acc[s - 1], row >> s, [(before, mine), (got[s - 1], row >> s)], size)
+        if s <= 2:
+            size = count >> (s + 1)
+            source, first = (self.part, row) if s == 0 else (acc[s - 1], row >> s)
+            axis = order[s]
+            other = first + (1 - bit[axis]) * size
+            self.start(n, s, rows_of(source, other, size), rows_of(got[s], row >> (s + 1), size), peer[axis])
+        elif s == 3:
+            size = count >> 5
+            for i in range(3):
+                theirs = (row >> 3) + lax.rem(self.z + i + 1, 4) * size
+                target = rows_of(self.got_z.at[i], row >> 5, size)
+                self.start(n, 3 + i, rows_of(acc[2], theirs, size), target, self.z_peer[i])
+        elif s == 4:
+            size = count >> 5
+            for i in range(3):
+                self.open[n, 3 + i].wait_recv()
+            place = row
+            for level in range(3):
+                place = place + bit[order[level]] * (count >> (level + 1))
+            self.place[n] = place
+            mine = place + self.z * size
+            others = [(self.got_z.at[i], row >> 5) for i in range(3)]
+            add_rows(res, mine, [(acc[2], (row >> 3) + self.z * size), *others], size)
+            for i in range(3):
+                block = rows_of(res, mine, size)
+                self.start(n, 6 + i, block, block, self.z_peer[i])
+        elif s <= 7:
+            for slot in (6, 7, 8) if s == 5 else (s + 3,):
+                self.open[n, slot].wait_recv()
+            level = 7 - s
+            size = count >> (level + 1)
+            block = rows_of(res, self.place[n], size)
+            self.start(n, s + 4, block, block, peer[order[level]])
+            self.place[n] = self.place[n] - bit[order[level]] * size
+        else:
+            self.open[n, 11].wait_recv()
+            pltpu.make_async_copy(
+                rows_of(res, row, count), rows_of(self.out, row, count), self.out_sem.at[n]
+            ).start()
+
+    def finish(self, parts):
+        for copy in self.sends:
+            copy.wait_send()
+        for n, (row, count, _) in enumerate(parts):
+            pltpu.make_async_copy(
+                rows_of(self.res, row, count), rows_of(self.out, row, count), self.out_sem.at[n]
+            ).wait()
+
+
+def weights_body(remote, *refs):
+    left, right, left_post, right_post, rows_grad, stat_a, stat_b, depth_a, depth_b, out = refs[:10]
+    held_left, held_right, sums, part, load_sem = refs[10:15]
+    scratch = refs[15:]
+    tokens = right.shape[0]
+
+    def loads(k):
+        slot = k % 2
+        if k < 4:
+            pairs = [
+                (left.at[k * ALL : (k + 1) * ALL, :], held_left.at[slot, :ALL, :]),
+                (right.at[:, k * 4 * ALL : (k + 1) * 4 * ALL], held_right.at[slot]),
+            ]
+        elif k == 4:
+            pairs = [
+                (left.at[2 * D : 3 * D, :], held_left.at[slot, :D, :]),
+                (right.at[:, 2 * FF :], held_right.at[slot, :, :D]),
+            ]
+        elif k < 7:
+            first = 3 * D + (k - 5) * ALL
+            pairs = [
+                (left.at[first : first + ALL, :], held_left.at[slot, :ALL, :]),
+                (rows_grad, held_right.at[slot]),
+            ]
+        else:
+            pairs = [
+                (left_post, held_left.at[slot]),
+                (right_post, held_right.at[slot, :, :D]),
+            ]
+        return [
+            pltpu.make_async_copy(source, target, load_sem.at[slot, i])
+            for i, (source, target) in enumerate(pairs)
+        ]
+
+    def compute(k):
+        for copy in loads(k):
+            copy.wait()
+        if k + 1 < CHUNKS:
+            for copy in loads(k + 1):
+                copy.start()
+        slot = k % 2
+        by_left = {4: 2, 7: 1}.get(k, 4)
+
+        def unit(j, carry):
+            if by_left == 4:
+                a, b = 0, j
+            elif by_left == 2:
+                a, b = j // 2, lax.rem(j, 2)
+            else:
+                a, b = j, 0
+            lhs = held_left[slot, pl.ds(pl.multiple_of(a * ALL, ALL), ALL), :]
+            rhs = held_right[slot, :, pl.ds(pl.multiple_of(b * ALL, ALL), ALL)]
+            value = nn(lhs, rhs)
+            for c in range(3):
+                rows_of(part, k * CHUNK + j * UNIT + c * ALL, ALL)[...] = value[
+                    :, c * 128 : (c + 1) * 128
+                ].astype(BF)
+            return carry
+
+        lax.fori_loop(0, 2 if k == 7 else 4, unit, 0)
+        ones = jnp.ones((16, tokens), BF)
+        if k in (0, 1, 4, 5):
+            wide = 2 if k == 4 else 4
+            first = {0: 28, 1: 32, 4: 36, 5: 38}[k]
+            total = nn(ones, held_right[slot, :, : wide * ALL])
+            for j in range(wide):
+                sums[first + j : first + j + 1, :] = total[0:1, j * ALL : (j + 1) * ALL]
+        if k == 7:
+            span = nn(held_left[slot, D:, :], held_right[slot, :, ALL:D])
+            for c in range(3):
+                part[SPAN_ROW + c * 128 : SPAN_ROW + (c + 1) * 128, :] = span[
+                    :, c * 128 : (c + 1) * 128
+                ].astype(BF)
+            sums[42:43, :] = nn(ones, held_right[slot, :, :ALL])[0:1]
+            sums[43:44, :128] = nt(ones, held_left[slot, D:, :])[0:1]
+            for first, a, b in ((0, stat_a, stat_b), (10, depth_a, depth_b)):
+                for i in range(a.shape[0] // 8):
+                    both = jnp.sum(a[i * 8 : i * 8 + 8] + b[i * 8 : i * 8 + 8], axis=0, keepdims=True)
+                    sums[first + 2 * i : first + 2 * i + 1, :] = both[:, :ALL]
+                    sums[first + 2 * i + 1 : first + 2 * i + 2, :] = both[:, ALL:]
+            small = sums[...].astype(BF)
+            for c in range(3):
+                part[SMALL_ROW + c * SMALL : SMALL_ROW + (c + 1) * SMALL, :] = small[
+                    :, c * 128 : (c + 1) * 128
+                ]
+            part[SMALL_ROW + 3 * SMALL :, :] = jnp.zeros((PACKED - SMALL_ROW - 3 * SMALL, 128), BF)
+
+    for copy in loads(0):
+        copy.start()
+    sums[...] = jnp.zeros_like(sums)
+    if not remote:
+        for k in range(CHUNKS):
+            compute(k)
+        pltpu.sync_copy(part, out)
+        return
+    res, *scratch = scratch
+    exchange = Exchange(part, res, out, scratch)
+    exchange.greet()
+    parts = [p for k in range(CHUNKS) for p in chunk_parts(k)]
+    for t in range(CHUNKS + 8):
+        if t < CHUNKS:
+            compute(t)
+        if t == 0:
+            exchange.await_greetings()
+        for k in range(CHUNKS):
+            if 0 <= t - k <= 8:
+                for n in (2 * k, 2 * k + 1):
+                    exchange.stage(n, parts[n], t - k)
+    exchange.finish(parts)
+
+
+def weights_call(remote, big, small):
+    tokens = big[1].shape[0]
+    n_parts = 2 * CHUNKS
+    scratch = [
+        pltpu.VMEM((2, D + 128, tokens), BF),
+        pltpu.VMEM((2, tokens, 4 * ALL), BF),
+        pltpu.VMEM((SMALL, ALL), F32),
+        pltpu.VMEM((PACKED, 128), BF),
+        pltpu.SemaphoreType.DMA((2, 2)),
+    ]
+    if remote:
+        scratch += [
+            pltpu.VMEM((PACKED, 128), BF),
+            pltpu.VMEM((PACKED >> 1, 128), BF),
+            pltpu.VMEM((PACKED >> 2, 128), BF),
+            pltpu.VMEM((PACKED >> 3, 128), BF),
+            pltpu.VMEM((3, PACKED >> 5, 128), BF),
+            pltpu.VMEM((PACKED >> 1, 128), BF),
+            pltpu.VMEM((PACKED >> 2, 128), BF),
+            pltpu.VMEM((PACKED >> 3, 128), BF),
+            pltpu.SemaphoreType.DMA((n_parts, 12)),
+            pltpu.SemaphoreType.DMA((n_parts, 12)),
+            pltpu.SemaphoreType.DMA((n_parts,)),
+        ]
+    more = dict(collective_id=0, has_side_effects=True) if remote else {}
     return pl.pallas_call(
-        functools.partial(grad_body, flip, sums),
-        grid=(groups, tiles),
+        functools.partial(weights_body, remote),
+        in_specs=[pl.BlockSpec(memory_space=pl.ANY)] * len(big)
+        + [pl.BlockSpec(memory_space=pltpu.VMEM)] * len(small),
+        out_specs=pl.BlockSpec(memory_space=pl.ANY),
+        out_shape=jax.ShapeDtypeStruct((PACKED, 128), BF),
+        scratch_shapes=scratch,
+        compiler_params=params(**more),
+        cost_estimate=pl.CostEstimate(
+            flops=2 * 31 * ALL * ALL * tokens, bytes_accessed=50_000_000, transcendentals=0
+        ),
+        name="weights",
+    )(*big, *small)
+
+
+SMALL_OUTS = [
+    ("gain_second", 0, D),
+    ("shift_second", 2, D),
+    ("gain_first", 4, D),
+    ("shift_first", 6, D),
+    ("bias_outer", 8, D),
+    ("bias_inner", 28, FF),
+    ("bias_output", 36, D),
+    ("bias_unfold", 38, ALL),
+    ("bias_query", 39, ALL),
+    ("bias_value", 41, ALL),
+    ("bias_point", 42, ALL),
+    ("bias_span", 43, TAPS),
+]
+
+
+def unpack_body(unit, tail, inner, outer, output, unfold, project, point, span, depth, *small):
+    step = pl.program_id(0)
+
+    def tile():
+        return jnp.concatenate([unit[c * ALL : (c + 1) * ALL, :] for c in range(3)], axis=1)
+
+    @pl.when(step < 8)
+    def _():
+        inner[0] = tile().astype(F32)
+
+    @pl.when((step >= 8) & (step < 16))
+    def _():
+        outer[0] = tile().T.astype(F32)
+
+    @pl.when((step >= 16) & (step < 20))
+    def _():
+        output[...] = tile().astype(F32)
+
+    @pl.when((step == 20) | (step == 24))
+    def _():
+        unfold[...] = tile().astype(F32)
+
+    @pl.when((step > 20) & (step < 28) & (step != 24))
+    def _():
+        project[...] = tile().astype(F32)
+
+    @pl.when(step >= 28)
+    def _():
+        point[...] = tile().astype(F32)
+
+    @pl.when(step == 29)
+    def _():
+        wide = jnp.concatenate([tail[c * 128 : (c + 1) * 128, :] for c in range(3)], axis=1)
+        span[...] = wide.astype(F32).T[:, :TAPS]
+        rows = jnp.concatenate(
+            [tail[ALL + c * SMALL : ALL + (c + 1) * SMALL, :] for c in range(3)], axis=1
+        ).astype(F32)
+        for j in range(KERNEL):
+            for half in range(2):
+                depth[j : j + 1, half * ALL : (half + 1) * ALL] = rows[10 + 2 * j + half :][:1]
+        for ref, (_, first, size) in zip(small, SMALL_OUTS):
+            for i in range(max(1, size // ALL)):
+                wide = min(size, ALL)
+                ref[i * ALL : i * ALL + wide] = rows[first + i, :wide]
+
+
+def unpack_call(packed):
+    def span_of(first, count):
+        return lambda s: jnp.clip(s - first, 0, count - 1)
+
+    inner_at, outer_at, output_at, rows_at, point_at = (
+        span_of(*v) for v in ((0, 8), (8, 8), (16, 4), (20, 8), (28, 2))
+    )
+    square = (ALL, ALL)
+    specs = [
+        ((GROUPS, ALL, 4 * ALL), pl.BlockSpec((1, ALL, ALL), lambda s: (inner_at(s) // 4, 0, inner_at(s) % 4))),
+        ((GROUPS, 4 * ALL, ALL), pl.BlockSpec((1, ALL, ALL), lambda s: (outer_at(s) // 4, outer_at(s) % 4, 0))),
+        ((D, D), pl.BlockSpec(square, lambda s: (output_at(s) // 2, output_at(s) % 2))),
+        ((D, ALL), pl.BlockSpec(square, lambda s: (rows_at(s) // 4, 0))),
+        ((D, 3 * ALL), pl.BlockSpec(square, lambda s: (rows_at(s) // 4, jnp.maximum(rows_at(s) % 4 - 1, 0)))),
+        ((D, ALL), pl.BlockSpec(square, lambda s: (point_at(s), 0))),
+        ((ALL, TAPS), pl.BlockSpec((ALL, TAPS), lambda s: (0, 0))),
+        ((KERNEL, D), pl.BlockSpec((KERNEL, D), lambda s: (0, 0))),
+    ]
+    specs += [((size,), pl.BlockSpec((size,), lambda s: (0,))) for _, _, size in SMALL_OUTS]
+    tail = 768
+    return pl.pallas_call(
+        unpack_body,
+        grid=(30,),
         in_specs=[
-            pl.BlockSpec((high, n_long), lambda g, t: (g, 0)),
-            pl.BlockSpec((high, n_short), lambda g, t: (g, 0)),
-            pl.BlockSpec((n_long, tile), lambda g, t: (0, g * tiles + t)),
-            pl.BlockSpec((n_short, tile), lambda g, t: (0, g * tiles + t)),
+            pl.BlockSpec((UNIT, 128), lambda s: (s, 0)),
+            pl.BlockSpec((tail, 128), lambda s: (SPAN_ROW // tail, 0)),
         ],
-        out_specs=out_specs,
-        out_shape=out_shape,
+        out_specs=[b for _, b in specs],
+        out_shape=[jax.ShapeDtypeStruct(s, F32) for s, _ in specs],
         compiler_params=params(),
-        cost_estimate=pl.CostEstimate(
-            flops=2 * groups * high * wide * (n_long + n_short),
-            bytes_accessed=4_000_000,
-            transcendentals=0,
-        ),
-        name=name,
-    )(*left, *right)
+        cost_estimate=pl.CostEstimate(flops=0, bytes_accessed=27_000_000, transcendentals=0),
+        name="unpack",
+    )(packed, packed)
 
 
 def shards(
@@ -667,78 +1013,59 @@
     *short_kept, short_mixed = pre_call([short_x], pre_consts)
     *long_kept, long_mixed = pre_call(xs, pre_consts)
 
-    f_long = ffn_call(None, long_mixed, long_input, long_cotan, ffn_consts)
-    f_short = ffn_call(live_slots, short_mixed, short_x, short_cot, ffn_consts)
-    (l_out, l_fig, l_mg, l_act, l_inl, l_al, l_flt, l_olt, l_mixt, l_xt, l_stat) = f_long
-    (s_out, s_fig, s_mg, s_act, s_inl, s_al, s_flt, s_olt, s_mixt, s_xt, s_stat) = f_short
-
+    tokens = (long_input.shape[0] + short_x.shape[0]) * short_x.shape[1]
+    l_out, l_fig, l_mg, *joint, l_stat = ffn_call(
+        None, long_mixed, long_input, long_cotan, ffn_consts, (), tokens
+    )
+    s_out, s_fig, s_mg, left, right, s_stat = ffn_call(
+        live_slots, short_mixed, short_x, short_cot, ffn_consts, joint, tokens
+    )
     post_consts = (vec, w_point, w_span, spread, perm)
-    l_post = post_call(xs, l_mg, l_fig, long_kept, post_consts)
-    (l_pl, l_ll, l_dlt, l_spt, l_dkg), l_rest = l_post[:5], l_post[5:]
-    own, far, (l_qt, l_ug, l_tg) = l_rest[0], l_rest[1:n_blk], l_rest[n_blk:]
+    l_post = post_call(xs, l_mg, l_fig, long_kept, post_consts, (), tokens)
+    (*joint, l_dkg, own), l_rest = l_post[:4], l_post[4:]
+    far, (l_qt, l_ug, l_tg) = l_rest[: n_blk - 1], l_rest[n_blk - 1 :]
     far = [
         lax.ppermute(a, "blk", [(i, (i - k) % n_blk) for i in range(n_blk)])
         for k, a in enumerate(far, 1)
     ]
-    s_post = post_call([short_x], s_mg, s_fig, short_kept, post_consts + (w_project, w_unfold))
-    s_pl, s_ll, s_dlt, s_spt, s_dkg, short_grad, s_ru = s_post
-    w_inner_grad, inner_sums = grad_call((l_flt, s_flt), (l_inl, s_inl), 512, 2, False, True, "grad_inner")
-    (w_outer_grad,) = grad_call((l_olt, s_olt), (l_act, s_act), 512, 2, True, False, "grad_outer")
-    w_output_grad, output_sums = grad_call((l_mixt, s_mixt), (l_al, s_al), 256, 1, False, True, "grad_output")
-    w_point_grad, point_sums = grad_call((l_dlt, s_dlt), (l_pl, s_pl), 128, 1, False, True, "grad_point")
-    w_span_grad, span_sums = grad_call((l_spt, s_spt), (l_ll, s_ll), 128, 1, False, True, "grad_span")
-    long_grad, l_ru = end_call(own, far, l_qt, l_ug, l_tg, w_project, w_unfold)
-    ru_grad, ru_sums = grad_call((l_xt, s_xt), (l_ru, s_ru), 256, 1, False, True, "grad_rows")
-
-    stat = (l_stat + s_stat).reshape(5, 8, D).sum(1)
-    dkg = (l_dkg + s_dkg).reshape(KERNEL, 8, D).sum(1)
-    small = jnp.concatenate(
-        [
-            stat.reshape(-1),
-            dkg.reshape(-1),
-            inner_sums[0],
-            output_sums[0],
-            point_sums[0],
-            span_sums[0],
-            ru_sums[0],
-        ]
+    left_post, right_post, s_dkg, short_grad, rows_grad = post_call(
+        [short_x], s_mg, s_fig, short_kept, post_consts + (w_project, w_unfold), joint, tokens
     )
-    axes = ("dp", "blk")
-    small = lax.psum(small, axes)
-    big = lax.psum((w_inner_grad, w_outer_grad, w_output_grad, w_point_grad, w_span_grad, ru_grad), axes)
-    w_inner_grad, w_outer_grad, w_output_grad, w_point_grad, w_span_grad, ru_grad = (
-        b.astype(F32) for b in big
+    long_grad, rows_grad = end_call(own, far, l_qt, l_ug, l_tg, w_project, w_unfold, rows_grad)
+
+    remote = lax.axis_size("dp") == 8 and n_blk == 4
+    packed = weights_call(
+        remote, (left, right, left_post, right_post, rows_grad), (l_stat, s_stat, l_dkg, s_dkg)
     )
-    sizes = [D] * 5 + [KERNEL * D, FF, D, ALL, 128, ALL, ALL, ALL, ALL]
-    places = np.cumsum([0] + sizes)
-    (gs, ss, gf, sf, bo, dk, bi, bout, bp, bs, bu, bq, _, bv) = (
-        small[a:b] for a, b in zip(places[:-1], places[1:])
-    )
+    if not remote:
+        packed = lax.psum(packed, ("dp", "blk"))
+    inner, outer, output, unfold, project, point, span, depth, *small = unpack_call(packed)
+    named = {name: value for (name, _, _), value in zip(SMALL_OUTS, small)}
     return (
         l_out,
         s_out.reshape(short_input.shape),
         long_grad,
         short_grad.reshape(short_input.shape),
-        ru_grad[0][:, ALL:],
-        bq,
-        bv,
-        dk.reshape(KERNEL, D),
-        w_point_grad[0],
-        bp,
-        w_span_grad[0][:, :TAPS],
-        bs[:TAPS],
-        ru_grad[0][:, :ALL],
-        bu,
-        w_output_grad[0],
-        bout,
-        gf,
-        sf,
-        w_inner_grad,
-        bi,
-        w_outer_grad,
-        bo,
-        gs,
-        ss,
+        project,
+        named["bias_query"],
+        named["bias_value"],
+        depth,
+        point,
+        named["bias_point"],
+        span,
+        named["bias_span"],
+        unfold,
+        named["bias_unfold"],
+        output,
+        named["bias_output"],
+        named["gain_first"],
+        named["shift_first"],
+        inner,
+        named["bias_inner"],
+        outer,
+        named["bias_outer"],
+        named["gain_second"],
+        named["shift_second"],
     )
 
 

time: 573 us -> 319 us (0.56)
  waiting for transfers between devices: 302 us -> 0.02 us
  Pallas kernels: 208 us -> 294 us
  local copies, waits for them, and re-layouts: 31.5 us -> 16 us
  between operations: 14.9 us -> 1.45 us
  other arithmetic: 8.11 us -> 0 us
    psum x2 -> x0, waiting for transfers between devices: 301 us -> none  [the longest x1 190 us: shards(): lax.psum((w_inner_grad, w_outer_grad, w_output_grad, w_point_grad, w_span...]
    pallas_call x6 -> x2, Pallas kernels: 40.8 us -> 128 us  [the longest x1 105 us: weights_call(): pl.pallas_call(functools.partial(weights_body, remote), in_specs=[pl.Bloc...]
    slice x11 -> x0, local copies, waits for them, and re-layouts: 13.6 us -> none  [the longest x4 4.86 us: shards(): small[a:b]]
  transfers between devices with their start and end apart: 8 -> 6, of which waited for: 3 -> 0; matrix products, arithmetic and copies ran while one was open for 4% -> 4% of each run, Pallas kernels for 24% -> 33%
where the time goes in v2:
time: 319 us; the launch traced here: 317 us
  Pallas kernels  294 us (92%)
  local copies, waits for them, and re-layouts  16 us (5%)
  starting transfers between devices  6.29 us (2%)
    pallas_call x1, Pallas kernels, weights_call(): pl.pallas_call(functools.partial(weights_body, remote), in_specs=[pl.Bloc...  105 us
    pallas_call x2, Pallas kernels, ffn_call(): pl.pallas_call(functools.partial(ffn_body, masked), grid=(count,), in_spe...  63.4 us
    pallas_call x2, Pallas kernels, post_call(): pl.pallas_call(functools.partial(post_body, len(xs)), grid=(count,), in_s...  53.2 us
    pallas_call x2, Pallas kernels, pre_call(): pl.pallas_call(functools.partial(pre_body, len(xs)), grid=(count,), in_sp...  42.4 us
    pallas_call x1, Pallas kernels, unpack_call(): pl.pallas_call(unpack_body, grid=(30,), in_specs=[pl.BlockSpec((UNIT, 128...  22.5 us
    concatenate x1, local copies, waits for them, and re-layouts, shards(): jnp.concatenate([bias_query, bias_value, bias_point, bias_unfold, bias_ou...  8.32 us
    pallas_call x1, Pallas kernels, end_call(): pl.pallas_call(functools.partial(end_body, 1 + len(far)), grid=(count,),...  6.73 us
  transfers between devices with their start and end apart: 6, of which 0 were waited for; matrix products, arithmetic and copies ran while one was open for 4% of the time, Pallas kernels for 33%

profile of v2, /device:TPU:1, one launch (start us, length us, event | category | flops | bytes accessed | tf_op | source)
XLA Modules:
  0.0 317.4 jit_solution(7044366486504313457)
XLA Ops:
  0.8 2.7 collective-permute-start.1
  3.4 1.3 collective-permute-start
  5.4 0.8 reshape.66
  6.2 8.3 %concatenate.3 = bf16[18432]{0:T(1024)(128)(2,1)S(1)} concatenate(bf16[384]{0:T(512)(128)(2,1)} %param.33, bf16[384]{0:T(512)(128)(2,1)} %param.34, bf16[384]{0:T(512)(128)(2,1)} %param.37, bf16[384]{0:T(512)(128)(2,1)} %param.41, bf16[768]{0:T(1024)(128)(2,1)} %param.43, bf16[768]{0:T(1024)(128)(2,1)} %param.44, bf16[768]{0:T(1024)(128)(2,1)} %param.45, bf16[768]{0:T(1024)(128)(2,1)} %param.49, ...), dimensions={0} | concatenate | bytes 73728 | tf_op jit(solution)/shard_map/concatenate | solution.py:988
  14.5 0.7 reshape.71.refs_4_.refs_3_.refs_1_.refs_14_.refs_11_
  15.2 1.5 copy.56.refs_7_.refs_4_.refs_16_.refs_13_
  16.7 26.3 %pre_short.1 = (bf16[8,128,384]{2,1,0:T(8,128)(2,1)}, bf16[8,128,384]{2,1,0:T(8,128)(2,1)}, bf16[8,128,384]{2,1,0:T(8,128)(2,1)}, bf16[8,3,256,128]{3,2,1,0:T(8,...) custom-call(bf16[8,128,768]{2,1,0:T(8,128)(2,1)} %bitcast.5, ...), custom_call_target="tpu_custom_call" | custom-call | flops 6144000000 | bytes 20000000 | tf_op jit(solution)/shard_map/pre_short/pallas_call | solution.py:208
  43.1 0.8 copy-done.3
  43.9 0.2 copy-done.4
  44.1 0.8 copy-done.5
  44.9 16.1 %pre_long.1 = (bf16[3,128,384]{2,1,0:T(8,128)(2,1)}, bf16[3,512,384]{2,1,0:T(8,128)(2,1)}, bf16[3,512,384]{2,1,0:T(8,128)(2,1)}, bf16[3,3,1024,128]{3,2,1,0:T(8,...) custom-call(bf16[3,128,768]{2,1,0:T(8,128)(2,1)} %refs_0_.4, ...), custom_call_target="tpu_custom_call" | custom-call | flops 2304000000 | bytes 20000000 | tf_op jit(solution)/shard_map/pre_long/pallas_call | solution.py:208
  61.0 19.4 %ffn_long.1 = (bf16[3,128,768]{2,1,0:T(8,128)(2,1)}, f32[3,128,768]{2,1,0:T(8,128)}, bf16[3,128,768]{2,1,0:T(8,128)(2,1)}, bf16[3072,1408]{1,0:T(8,128)(2,1)}, b...) custom-call(bf16[3,128,768]{2,1,0:T(8,128)(2,1)} %get-tuple-element.91.refs_0_, bf16[3,128,768]{2,1,0:T(8,128)(2,1)} %refs_0_.4, ...), custom_call_target="tpu_custom_call" | custom-call | flops 4608000000 | bytes 30000000 | tf_op jit(solution)/shard_map/ffn_long/pallas_call | solution.py:330
  80.4 17.8 %post_long.1 = (bf16[896,1408]{1,0:T(8,128)(2,1)}, bf16[1408,768]{1,0:T(8,128)(2,1)}, f32[72,768]{1,0:T(8,128)}, f32[3,128,768]{2,1,0:T(8,128)}, bf16[3,144,768]...) custom-call(bf16[3,128,768]{2,1,0:T(8,128)(2,1)} %refs_0_.4, ...), custom_call_target="tpu_custom_call" | custom-call | flops 3840000000 | bytes 30000000 | tf_op jit(solution)/shard_map/post_long/pallas_call | solution.py:509
  98.1 0.4 collective-permute-start.4
  98.6 1.7 collective-permute-start.5
  100.3 44.0 %ffn_short.1 = (bf16[8,128,768]{2,1,0:T(8,128)(2,1)}, f32[8,128,768]{2,1,0:T(8,128)}, bf16[8,128,768]{2,1,0:T(8,128)(2,1)}, bf16[3072,1408]{1,0:T(8,128)(2,1)}, ...) custom-call(s32[1,1]{1,0:T(1,128)S(6)} %copy.66.refs_0_, ...), custom_call_target="tpu_custom_call", output_to_operand_aliasing={{3}: (8, {}), {4}: (9, {})} | custom-call | flops 12288000000 | bytes 30000000 | tf_op jit(solution)/shard_map/ffn_short/pallas_call | solution.py:330
  144.3 35.5 %post_short.1 = (bf16[896,1408]{1,0:T(8,128)(2,1)}, bf16[1408,768]{1,0:T(8,128)(2,1)}, f32[72,768]{1,0:T(8,128)}, f32[8,128,768]{2,1,0:T(8,128)}, bf16[1408,1536]{1,0:T(8,128)(2,1)}) custom-call(bf16[8,128,768]{2,1,0:T(8,128)(2,1)} %bitcast.7, bf16[8,128,768]{2,1,0:T(8,128)(2,1)} %get-tuple-element.114.refs_1_, ...), custom_call_target="tpu_custom_call", output_to_operand_aliasing={{0}: (18, {}), {1}: (19, {})} | custom-call | flops 10240000000 | bytes 30000000 | tf_op jit(solution)/shard_map/post_short/pallas_call | solution.py:509
  179.9 0.8 copy-done.2
  180.6 0.2 copy-done
  180.9 0.2 copy-done.1
  181.1 6.7 %end_long.1 = (f32[3,128,768]{2,1,0:T(8,128)}, bf16[1408,1536]{1,0:T(8,128)(2,1)}) custom-call(f32[3,128,768]{2,1,0:T(8,128)} %get-tuple-element.107.refs_0_, bf16[3,144,768]{2,1,0:T(8,128)(2,1)} %copy-done, bf16[3,128,768]{2,1,0:T(8,128)(2,1)} %copy-done.2, bf16[3,144,768]{2,1,0:T(8,128)(2,1)} %copy-done.1, ...), custom_call_target="tpu_custom_call", output_to_operand_aliasing={{1}: (9, {})} | custom-call | flops 921600000 | bytes 10000000 | tf_op jit(solution)/shard_map/end_long/pallas_call | solution.py:554
  187.8 105.4 %weights.1.unit.tail = bf16[35328,128]{1,0:T(8,128)(2,1)} custom-call(bf16[3072,1408]{1,0:T(8,128)(2,1)} %get-tuple-element.129.refs_0_, bf16[1408,6912]{1,0:T(8,128)(2,1)} %get-tuple-element.130.refs_1_, bf16[896,1408]{1,0:T(8,128)(2,1)} %get-tuple-element.131.refs_2_, bf16[1408,768]{1,0:T(8,128)(2,1)} %get-tuple-element.132.refs_3_, ...), custom_call_target="tpu_custom_call" | custom-call | flops 12872318976 | bytes 50000000 | tf_op jit(solution)/shard_map/weights/pallas_call | solution.py:846
  293.2 22.5 %unpack.1 = (f32[2,384,1536]{2,1,0:T(8,128)}, f32[2,1536,384]{2,1,0:T(8,128)}, f32[768,768]{1,0:T(8,128)}, f32[768,384]{1,0:T(8,128)}, f32[768,1152]{1,0:T(8,128...) custom-call(bf16[35328,128]{1,0:T(8,128)(2,1)} %weights.1.unit.tail,, ...), custom_call_target="tpu_custom_call" | custom-call | bytes 27000000 | tf_op jit(solution)/shard_map/unpack/pallas_call | solution.py:943
  315.7 1.7 copy.60
  (15 shorter events, 0.2 us)
Async XLA Ops:
  0.7 42.4 %collective-permute-start.2 = (bf16[3,128,768]{2,1,0:T(8,128)(2,1)}, bf16[3,128,768]{2,1,0:T(8,128)(2,1)S(1)}, u32[]{:S(2)}, u32[]{:S(2)}) collective-permute-start(bf16[3,128,768]{2,1,0:T(8,128)(2,1)} %refs_0_.4), channel_id=1, source_target_pairs={{0,3},{1,0},{2,1},{3,2},{4,7},{5,4},{6,5},{7,6},{8,11},{9,8},{10,9... | collective-permute-start | bytes 1769480 | tf_op jit(solution)/shard_map/ppermute | solution.py:1008
  0.8 42.3 %collective-permute-start.1 = (bf16[3,128,768]{2,1,0:T(8,128)(2,1)}, bf16[3,128,768]{2,1,0:T(8,128)(2,1)S(1)}, u32[]{:S(2)}, u32[]{:S(2)}) collective-permute-start(bf16[3,128,768]{2,1,0:T(8,128)(2,1)} %refs_0_.4), channel_id=1, source_target_pairs={{0,2},{1,3},{2,0},{3,1},{4,6},{5,7},{6,4},{7,5},{8,10},{9,11},{10,... | collective-permute-start | bytes 1769480 | tf_op jit(solution)/shard_map/ppermute | solution.py:1008
  3.4 39.7 %collective-permute-start = (bf16[3,128,768]{2,1,0:T(8,128)(2,1)}, bf16[3,128,768]{2,1,0:T(8,128)(2,1)S(1)}, u32[]{:S(2)}, u32[]{:S(2)}) collective-permute-start(bf16[3,128,768]{2,1,0:T(8,128)(2,1)} %refs_0_.4), channel_id=1, source_target_pairs={{0,1},{1,2},{2,3},{3,0},{4,5},{5,6},{6,7},{7,4},{8,9},{9,10},{10,1... | collective-permute-start | bytes 1769480 | tf_op jit(solution)/shard_map/ppermute | solution.py:1008
  43.1 0.8 copy-start.3
  43.1 1.0 copy-start.4
  44.1 0.8 copy-start.5
  98.1 81.7 %collective-permute-start.4 = (bf16[3,128,768]{2,1,0:T(8,128)(2,1)}, bf16[3,128,768]{2,1,0:T(8,128)(2,1)S(1)}, u32[]{:S(2)}, u32[]{:S(2)}) collective-permute-start(bf16[3,128,768]{2,1,0:T(8,128)(2,1)} %get-tuple-element.109), channel_id=1, source_target_pairs={{0,2},{1,3},{2,0},{3,1},{4,6},{5,7},{6,4},{7,5},{8,10},{9,11},{10,... | collective-permute-start | bytes 1769480 | tf_op jit(solution)/shard_map/ppermute | solution.py:1028
  98.6 81.3 %collective-permute-start.3 = (bf16[3,144,768]{2,1,0:T(8,128)(2,1)}, bf16[3,144,768]{2,1,0:T(8,128)(2,1)S(1)}, u32[]{:S(2)}, u32[]{:S(2)}) collective-permute-start(bf16[3,144,768]{2,1,0:T(8,128)(2,1)} %get-tuple-element.108), channel_id=1, source_target_pairs={{0,3},{1,0},{2,1},{3,2},{4,7},{5,4},{6,5},{7,6},{8,11},{9,8},{10,9... | collective-permute-start | bytes 1990664 | tf_op jit(solution)/shard_map/ppermute | solution.py:1028
  98.6 81.2 %collective-permute-start.5 = (bf16[3,144,768]{2,1,0:T(8,128)(2,1)}, bf16[3,144,768]{2,1,0:T(8,128)(2,1)S(1)}, u32[]{:S(2)}, u32[]{:S(2)}) collective-permute-start(bf16[3,144,768]{2,1,0:T(8,128)(2,1)} %get-tuple-element.110), channel_id=1, source_target_pairs={{0,1},{1,2},{2,3},{3,0},{4,5},{5,6},{6,7},{7,4},{8,9},{9,10},{10,1... | collective-permute-start | bytes 1990664 | tf_op jit(solution)/shard_map/ppermute | solution.py:1028
  179.8 0.8 copy-start.2
  179.8 1.0 copy-start
  179.9 1.2 copy-start.1

commit v3 on v2

--- a/solution.py
+++ b/solution.py
@@ -23,6 +23,7 @@
 BF = jnp.bfloat16
 ROOT_HALF = 0.7071067811865476
 DENSITY = 0.3989422804014327
+FFN_ROWS = 256
 VMEM_BYTES = 58 * 1024 * 1024
 
 
@@ -78,15 +79,17 @@
 
 
 def fill_ends(xp, x_refs, rows, sides):
-    if sides is None:
-        zero = jnp.zeros((8, D), F32)
-        xp[0:8, :] = zero
-        xp[8 + rows : 16 + rows, :] = zero
-    else:
-        lower, upper = sides
-        xp[0:8, :] = x_refs[1][0, rows - 16 :, :].astype(F32)[8:] * lower
-        xp[8 + rows : 16 + rows, :] = x_refs[-1][0, :16, :].astype(F32)[:8] * upper
-    xp[8 : 8 + rows, :] = x_refs[0][0].astype(F32)
+    for c in range(D // 128):
+        cols = slice(c * 128, (c + 1) * 128)
+        if sides is None:
+            zero = jnp.zeros((8, 128), F32)
+            xp[c, 0:8, :] = zero
+            xp[c, 8 + rows : 16 + rows, :] = zero
+        else:
+            lower, upper = sides
+            xp[c, 0:8, :] = x_refs[1][0, rows - 16 :, cols].astype(F32)[8:] * lower
+            xp[c, 8 + rows : 16 + rows, :] = x_refs[-1][0, :16, cols].astype(F32)[:8] * upper
+        xp[c, 8 : 8 + rows, :] = x_refs[0][0, :, cols].astype(F32)
 
 
 def row_sides():
@@ -95,11 +98,27 @@
     return (place > 0).astype(F32), (place < count - 1).astype(F32)
 
 
+def as_row(ref):
+    return ref[...].astype(F32).reshape(1, ref.shape[0])
+
+
 def pre_body(n_x, *refs):
-    x_refs = refs[:n_x]
-    vec, w_project, w_point, w_span, w_unfold, spread, perm = refs[n_x : n_x + 7]
-    q_out, k_out, v_out, p_out, kc_out, ker_out, dl_out, up_out, mix_out = refs[n_x + 7 : n_x + 16]
-    (xp,) = refs[n_x + 16 :]
+    x_refs, refs = refs[:n_x], refs[n_x:]
+    bias_query, bias_value, bias_point, bias_span, bias_unfold, depth_kernel = refs[:6]
+    w_project, w_point, w_span, w_unfold, spread, perm = refs[6:12]
+    q_out, k_out, v_out, p_out, kc_out, ker_out, dl_out, up_out, mix_out = refs[12:21]
+    xp, vec = refs[21:]
+
+    @pl.when(pl.program_id(0) == 0)
+    def _():
+        vec[16:24, :] = jnp.zeros((8, D), F32)
+        vec[0:1, :ALL] = as_row(bias_query)
+        vec[0:1, ALL:] = as_row(bias_value)
+        vec[1:2, :ALL] = as_row(bias_point)
+        vec[1:2, ALL:] = as_row(bias_unfold)
+        vec[21:22, :TAPS] = as_row(bias_span)
+        vec[8:17, :] = depth_kernel[...].astype(F32)
+
     rows = x_refs[0].shape[1]
     is_long = n_x > 1
     sides = row_sides() if is_long else None
@@ -122,14 +141,14 @@
 
     for c in range(D // 128):
         cols = slice(c * 128, (c + 1) * 128)
-        total = vec[12:13, cols] * xp[4 : 4 + rows, cols]
+        total = vec[8:9, cols] * xp[c, 4 : 4 + rows, :]
         for j in range(1, KERNEL):
-            total += vec[12 + j : 13 + j, cols] * xp[4 + j : 4 + j + rows, cols]
+            total += vec[8 + j : 9 + j, cols] * xp[c, 4 + j : 4 + j + rows, :]
         dl_out[0, :, cols] = total.astype(BF)
     key_conv = nn(dl_out[0], w_point[...]) + vec[1:2, :ALL]
     kc_out[0] = key_conv
     span = (key_conv * q.astype(F32)).astype(BF)
-    span_weights = nn(w_span[...], perm[:TAPS, :]).astype(BF)
+    span_weights = tn(w_span[...], perm[:TAPS, :]).astype(BF)
     span_bias = nn(vec[16:24, :128].astype(BF), perm[...])[5:6]
     logits = nn(span, span_weights) + span_bias
     lane = lax.broadcasted_iota(jnp.int32, (rows, 128), 1)
@@ -138,17 +157,22 @@
     ker_out[0] = kernel
 
     bias_unfold = vec[1:2, ALL:]
-    up_out[0, 8 : 8 + rows, :] = nn(x, w_unfold[...]) + bias_unfold
+    unfold_rows = nn(x, w_unfold[...]) + bias_unfold
+    for c in range(PAIRS):
+        up_out[0, c, 8 : 8 + rows, :] = unfold_rows[:, c * 128 : (c + 1) * 128]
     if is_long:
         lower, upper = sides
         ends = jnp.concatenate([x_refs[1][0, rows - 16 :, :], x_refs[-1][0, :16, :]], axis=0)
         unfold_ends = nn(ends, w_unfold[...]) + bias_unfold
-        up_out[0, 0:8, :] = unfold_ends[8:16] * lower
-        up_out[0, 8 + rows : 16 + rows, :] = unfold_ends[16:24] * upper
+        for c in range(PAIRS):
+            cols = slice(c * 128, (c + 1) * 128)
+            up_out[0, c, 0:8, :] = unfold_ends[8:16, cols] * lower
+            up_out[0, c, 8 + rows : 16 + rows, :] = unfold_ends[16:24, cols] * upper
     else:
-        zero = jnp.zeros((8, ALL), F32)
-        up_out[0, 0:8, :] = zero
-        up_out[0, 8 + rows : 16 + rows, :] = zero
+        zero = jnp.zeros((8, 128), F32)
+        for c in range(PAIRS):
+            up_out[0, c, 0:8, :] = zero
+            up_out[0, c, 8 + rows : 16 + rows, :] = zero
 
     low_half = lax.broadcasted_iota(jnp.int32, (1, 128), 1) < HEAD
     parts = two_parts(kernel)
@@ -157,9 +181,9 @@
     for p in range(PAIRS):
         cols = slice(p * 128, (p + 1) * 128)
         wide = nn(parts, spread[:, p * KERNEL * 128 : (p + 1) * KERNEL * 128])
-        total = wide[:, :128] * up_out[0, 4 : 4 + rows, cols]
+        total = wide[:, :128] * up_out[0, p, 4 : 4 + rows, :]
         for j in range(1, KERNEL):
-            total += wide[:, j * 128 : (j + 1) * 128] * up_out[0, 4 + j : 4 + j + rows, cols]
+            total += wide[:, j * 128 : (j + 1) * 128] * up_out[0, p, 4 + j : 4 + j + rows, :]
         mix_out[0, :, ALL + p * 128 : ALL + (p + 1) * 128] = total.astype(BF)
 
         scores = nt(head_stack(k_out[0, :, cols], low_half), scaled[:, cols])
@@ -202,7 +226,7 @@
         ((rows, ALL), F32),
         ((rows, 128), F32),
         ((rows, D), BF),
-        ((rows + 16, ALL), F32),
+        ((PAIRS, rows + 16, 128), F32),
         ((rows, D), BF),
     ]
     return pl.pallas_call(
@@ -211,7 +235,7 @@
         in_specs=[per_row(rows, D)] * len(xs) + [fixed(c) for c in consts],
         out_specs=[per_row(*s) for s, _ in shapes],
         out_shape=[jax.ShapeDtypeStruct((count, *s), t) for s, t in shapes],
-        scratch_shapes=[pltpu.VMEM((rows + 16, D), F32)],
+        scratch_shapes=[pltpu.VMEM((D // 128, rows + 16, 128), F32), pltpu.VMEM((24, D), F32)],
         compiler_params=params(),
         cost_estimate=pl.CostEstimate(
             flops=count * rows * 6_000_000, bytes_accessed=20_000_000, transcendentals=1_000_000
@@ -238,23 +262,17 @@
 
 
 def gelu_pair(v):
-    t = 1.0 / (1.0 + (0.3275911 * ROOT_HALF) * jnp.abs(v))
-    bell = jnp.exp(-0.5 * (v * v))
-    poly = 0.5 * 1.061405429
-    for term in (-1.453152027, 1.421413741, -0.284496736, 0.254829592):
-        poly = poly * t + 0.5 * term
-    tail = poly * t * bell
-    cdf = jnp.where(v >= 0, 1.0 - tail, tail)
-    return v * cdf, cdf + v * bell * DENSITY
-
-
-def ffn_body(masked, *refs):
+    cdf = 0.5 * (1.0 + lax.erf(v * ROOT_HALF))
+    return v * cdf, cdf + v * jnp.exp(-0.5 * (v * v)) * DENSITY
+
+
+def ffn_body(slot_rows, *refs):
+    masked = slot_rows > 0
     if masked:
         live_ref, *refs = refs
-        refs = refs[:7] + refs[9:]
-    (mix_ref, x_ref, cot_ref, vec, w_output, w_inner, w_outer) = refs[:7]
-    (out_ref, fig_ref, mg_ref, left, right, stat) = refs[7:13]
-    (slope,) = refs[13:]
+    mix_ref, x_ref, cot_ref = refs[:3]
+    vectors, (w_output, w_inner, w_outer) = refs[3:10], refs[10:13]
+    out_ref, fig_ref, mg_ref, left, right, stat, slope, vec = refs[-8:]
     inl_ref, act_ref = right.at[:, :FF], right.at[:, FF : 2 * FF]
     step = pl.program_id(0)
     rows = x_ref.shape[1]
@@ -262,6 +280,11 @@
     @pl.when(step == 0)
     def _():
         stat[...] = jnp.zeros_like(stat)
+        for i, ref in enumerate(vectors[:-1]):
+            vec[2 + i : 3 + i, :] = as_row(ref)
+        inner_row = as_row(vectors[-1])
+        for i in range(FF // D):
+            vec[8 + i : 9 + i, :] = inner_row[:, i * D : (i + 1) * D]
 
     x = x_ref[0]
     mixed = mix_ref[0]
@@ -288,7 +311,8 @@
     out_ref[0] = (second_normed * gain_second + vec[7:8, :]).astype(BF)
     seed = cot_ref[0].astype(F32)
     if masked:
-        seed = jnp.where(step < live_ref[0, 0], seed, 0.0)
+        token = step * rows + lax.broadcasted_iota(jnp.int32, (rows, 1), 0)
+        seed = jnp.where(token < live_ref[0, 0] * slot_rows, seed, 0.0)
     stat[0:8, :] += fold8(seed * second_normed)
     stat[8:16, :] += fold8(seed)
     second_grad = norm_back(seed, second_normed, second_inverse, gain_second)
@@ -312,11 +336,12 @@
     mg_ref[0] = nt(attended_low, w_output[...]).astype(BF)
 
 
-def ffn_call(live, mixed, x, cotan, consts, joint, tokens):
+def ffn_call(live, slot_rows, mixed, x, cotan, consts, joint, tokens):
     count, rows = x.shape[0], x.shape[1]
     total = count * rows
     masked = live is not None
-    first = tokens // rows - count if masked else 0
+    first = 0 if masked else tokens // rows - count
+    n_in = (4 if masked else 3) + len(consts)
     out_shapes = [
         ((count, rows, D), BF, per_row(rows, D)),
         ((count, rows, D), F32, per_row(rows, D)),
@@ -328,7 +353,7 @@
     head = [live] if masked else []
     head_specs = [pl.BlockSpec(memory_space=pltpu.SMEM)] if masked else []
     return pl.pallas_call(
-        functools.partial(ffn_body, masked),
+        functools.partial(ffn_body, slot_rows if masked else 0),
         grid=(count,),
         in_specs=head_specs
         + [per_row(rows, D)] * 3
@@ -336,8 +361,8 @@
         + [pl.BlockSpec(memory_space=pl.ANY)] * len(joint),
         out_specs=[s for _, _, s in out_shapes],
         out_shape=[jax.ShapeDtypeStruct(s, t) for s, t, _ in out_shapes],
-        scratch_shapes=[pltpu.VMEM((rows, FF), F32)],
-        input_output_aliases={8: 3, 9: 4} if masked else {},
+        scratch_shapes=[pltpu.VMEM((rows, FF), F32), pltpu.VMEM((16, D), F32)],
+        input_output_aliases={n_in: 3, n_in + 1: 4} if masked else {},
         compiler_params=params(),
         cost_estimate=pl.CostEstimate(
             flops=total * 12_000_000, bytes_accessed=30_000_000, transcendentals=total * FF
@@ -351,7 +376,7 @@
     x_refs = refs[:n_x]
     refs = refs[n_x:]
     (mg_ref, fig_ref, q_ref, k_ref, v_ref, p_ref, kc_ref, ker_ref, dl_ref, up_ref) = refs[:10]
-    (vec, w_point, w_span, spread, perm) = refs[10:15]
+    (depth_kernel, w_point, w_span, spread, perm) = refs[10:15]
     refs = refs[15:]
     if not is_long:
         (w_project, w_unfold), refs = refs[:2], refs[4:]
@@ -422,7 +447,7 @@
         wide = nn(parts, spread[:, table])
         products = []
         for j in range(KERNEL):
-            products.append((grad * up_ref[0, 4 + j : 4 + j + rows, cols]).astype(BF))
+            products.append((grad * up_ref[0, p, 4 + j : 4 + j + rows, :]).astype(BF))
             prp[j, 16 : 16 + rows, :] = wide[:, j * 128 : (j + 1) * 128] * grad
         kernel_grad += nt(jnp.concatenate(products, axis=1), spread[:128, table])
         first = 20 - ext
@@ -442,15 +467,16 @@
 
     logit_low = (kernel * (kernel_grad - window_sum(kernel * kernel_grad))).astype(BF)
     left[D:, :] = nt(perm[...], logit_low).astype(BF)
-    span_weights = nn(w_span[...], perm[:TAPS, :]).astype(BF)
-    span_grad = nt(logit_low, span_weights)
+    span_grad = nn(logit_low, tn(perm[:TAPS, :], w_span[...]).astype(BF))
     key_conv = kc_ref[0]
     right[:, ALL:] = (key_conv * qf).astype(BF)
     left[:D, :] = dl_ref[0].T
     point_low = (span_grad * qf).astype(BF)
     right[:, :ALL] = point_low
     query_total = (dq_scr[...] + span_grad * key_conv).astype(BF)
-    dgp[16 : 16 + rows, :] = nt(point_low, w_point[...])
+    depth_grad = nt(point_low, w_point[...])
+    for c in range(D // 128):
+        dgp[c, 16 : 16 + rows, :] = depth_grad[:, c * 128 : (c + 1) * 128]
 
     if not is_long:
         ru_out[:, ALL : 2 * ALL] = query_total
@@ -459,12 +485,12 @@
         qt_out[0] = query_total
     for c in range(D // 128):
         cols = slice(c * 128, (c + 1) * 128)
-        x_part = xp[:, cols] if is_long else x_refs[0][0, :, cols].astype(F32)
+        x_part = xp[c] if is_long else x_refs[0][0, :, cols].astype(F32)
         first = 20 - ext
         total = None
         for j in range(KERNEL):
-            moved = dgp[first - j : first - j + span_rows, cols]
-            term = vec[12 + j : 13 + j, cols] * moved
+            moved = dgp[c, first - j : first - j + span_rows, :]
+            term = depth_kernel[j : j + 1, cols].astype(F32) * moved
             total = term if total is None else total + term
             dkg[j * 8 : (j + 1) * 8, cols] += fold8(moved * x_part)
         if is_long:
@@ -480,7 +506,7 @@
     keys = rows * len(xs)
     total = count * rows
     is_long = len(xs) > 1
-    first = 0 if is_long else tokens // rows - count
+    first = tokens // rows - count if is_long else 0
     row_args = [mg, fig, *kept]
     outs = [
         ((D + 128, tokens), BF, pl.BlockSpec((D + 128, rows), lambda i: (0, first + i))),
@@ -494,14 +520,14 @@
         for i in range(1, len(xs)):
             outs.append(row_out(rows + 16 if i in (1, len(xs) - 1) else rows, D, BF))
         outs += [row_out(rows, ALL, BF), row_out(rows, ALL, F32), row_out(rows, D, F32)]
-        scratch.append(pltpu.VMEM((rows + 16, D), F32))
+        scratch.append(pltpu.VMEM((D // 128, rows + 16, 128), F32))
     else:
         outs += [
             row_out(rows, D, F32),
             ((tokens, 4 * ALL), BF, pl.BlockSpec((rows, 4 * ALL), lambda i: (first + i, 0))),
         ]
     scratch += [
-        pltpu.VMEM((rows + 32, D), F32),
+        pltpu.VMEM((D // 128, rows + 32, 128), F32),
         pltpu.VMEM((KERNEL, rows + 32, 128), F32),
         pltpu.VMEM((rows, ALL), F32),
     ]
@@ -550,13 +576,14 @@
 
 def end_call(own, far, qt, ug, tg, w_project, w_unfold, joint):
     count, rows = own.shape[0], own.shape[1]
+    first = joint.shape[0] // rows - count
     row_args = [own, *far, qt, ug, tg]
     return pl.pallas_call(
         functools.partial(end_body, 1 + len(far)),
         grid=(count,),
         in_specs=[per_row(*a.shape[1:]) for a in row_args]
         + [fixed(w_project), fixed(w_unfold), pl.BlockSpec(memory_space=pl.ANY)],
-        out_specs=[per_row(rows, D), pl.BlockSpec((rows, 4 * ALL), lambda i: (i, 0))],
+        out_specs=[per_row(rows, D), pl.BlockSpec((rows, 4 * ALL), lambda i: (first + i, 0))],
         out_shape=[
             jax.ShapeDtypeStruct((count, rows, D), F32),
             jax.ShapeDtypeStruct(joint.shape, BF),
@@ -874,46 +901,54 @@
 ]
 
 
-def unpack_body(unit, tail, inner, outer, output, unfold, project, point, span, depth, *small):
+def unpack_body(block, inner, outer, output, unfold, project, point, span, depth, *small):
     step = pl.program_id(0)
 
-    def tile():
-        return jnp.concatenate([unit[c * ALL : (c + 1) * ALL, :] for c in range(3)], axis=1)
-
-    @pl.when(step < 8)
+    def tile(unit):
+        start = unit * UNIT
+        return jnp.concatenate(
+            [block[start + c * ALL : start + (c + 1) * ALL, :] for c in range(3)], axis=1
+        )
+
+    @pl.when(step < 2)
     def _():
-        inner[0] = tile().astype(F32)
-
-    @pl.when((step >= 8) & (step < 16))
+        for i in range(4):
+            inner[0, :, i * ALL : (i + 1) * ALL] = tile(i).astype(F32)
+
+    @pl.when((step >= 2) & (step < 4))
     def _():
-        outer[0] = tile().T.astype(F32)
-
-    @pl.when((step >= 16) & (step < 20))
+        for i in range(4):
+            outer[0, i * ALL : (i + 1) * ALL, :] = tile(i).T.astype(F32)
+
+    @pl.when(step == 4)
     def _():
-        output[...] = tile().astype(F32)
-
-    @pl.when((step == 20) | (step == 24))
+        for i in range(4):
+            a, b = divmod(i, 2)
+            output[a * ALL : (a + 1) * ALL, b * ALL : (b + 1) * ALL] = tile(i).astype(F32)
+
+    @pl.when((step == 5) | (step == 6))
     def _():
-        unfold[...] = tile().astype(F32)
-
-    @pl.when((step > 20) & (step < 28) & (step != 24))
+        unfold[...] = tile(0).astype(F32)
+        for i in range(3):
+            project[:, i * ALL : (i + 1) * ALL] = tile(i + 1).astype(F32)
+
+    @pl.when(step == 7)
     def _():
-        project[...] = tile().astype(F32)
-
-    @pl.when(step >= 28)
-    def _():
-        point[...] = tile().astype(F32)
-
-    @pl.when(step == 29)
-    def _():
-        wide = jnp.concatenate([tail[c * 128 : (c + 1) * 128, :] for c in range(3)], axis=1)
-        span[...] = wide.astype(F32).T[:, :TAPS]
+        for i in range(2):
+            point[i * ALL : (i + 1) * ALL, :] = tile(i).astype(F32)
+        tail = 2 * UNIT
+        wide = jnp.concatenate(
+            [block[tail + c * 128 : tail + (c + 1) * 128, :] for c in range(3)], axis=1
+        )
+        span[...] = wide[:TAPS].astype(F32)
+        tail += ALL
         rows = jnp.concatenate(
-            [tail[ALL + c * SMALL : ALL + (c + 1) * SMALL, :] for c in range(3)], axis=1
+            [block[tail + c * SMALL : tail + (c + 1) * SMALL, :] for c in range(3)], axis=1
         ).astype(F32)
         for j in range(KERNEL):
             for half in range(2):
-                depth[j : j + 1, half * ALL : (half + 1) * ALL] = rows[10 + 2 * j + half :][:1]
+                place = 10 + 2 * j + half
+                depth[j : j + 1, half * ALL : (half + 1) * ALL] = rows[place : place + 1]
         for ref, (_, first, size) in zip(small, SMALL_OUTS):
             for i in range(max(1, size // ALL)):
                 wide = min(size, ALL)
@@ -921,38 +956,32 @@
 
 
 def unpack_call(packed):
-    def span_of(first, count):
+    def at(first, count):
         return lambda s: jnp.clip(s - first, 0, count - 1)
 
-    inner_at, outer_at, output_at, rows_at, point_at = (
-        span_of(*v) for v in ((0, 8), (8, 8), (16, 4), (20, 8), (28, 2))
-    )
-    square = (ALL, ALL)
+    inner_at, outer_at, rows_at = at(0, 2), at(2, 2), at(5, 2)
+    whole = lambda *shape: (shape, pl.BlockSpec(shape, lambda s: (0,) * len(shape)))
     specs = [
-        ((GROUPS, ALL, 4 * ALL), pl.BlockSpec((1, ALL, ALL), lambda s: (inner_at(s) // 4, 0, inner_at(s) % 4))),
-        ((GROUPS, 4 * ALL, ALL), pl.BlockSpec((1, ALL, ALL), lambda s: (outer_at(s) // 4, outer_at(s) % 4, 0))),
-        ((D, D), pl.BlockSpec(square, lambda s: (output_at(s) // 2, output_at(s) % 2))),
-        ((D, ALL), pl.BlockSpec(square, lambda s: (rows_at(s) // 4, 0))),
-        ((D, 3 * ALL), pl.BlockSpec(square, lambda s: (rows_at(s) // 4, jnp.maximum(rows_at(s) % 4 - 1, 0)))),
-        ((D, ALL), pl.BlockSpec(square, lambda s: (point_at(s), 0))),
-        ((ALL, TAPS), pl.BlockSpec((ALL, TAPS), lambda s: (0, 0))),
-        ((KERNEL, D), pl.BlockSpec((KERNEL, D), lambda s: (0, 0))),
+        ((GROUPS, ALL, 4 * ALL), pl.BlockSpec((1, ALL, 4 * ALL), lambda s: (inner_at(s), 0, 0))),
+        ((GROUPS, 4 * ALL, ALL), pl.BlockSpec((1, 4 * ALL, ALL), lambda s: (outer_at(s), 0, 0))),
+        whole(D, D),
+        ((D, ALL), pl.BlockSpec((ALL, ALL), lambda s: (rows_at(s), 0))),
+        ((D, 3 * ALL), pl.BlockSpec((ALL, 3 * ALL), lambda s: (rows_at(s), 0))),
+        whole(D, ALL),
+        whole(TAPS, ALL),
+        whole(KERNEL, D),
     ]
-    specs += [((size,), pl.BlockSpec((size,), lambda s: (0,))) for _, _, size in SMALL_OUTS]
-    tail = 768
+    specs += [whole(size) for _, _, size in SMALL_OUTS]
     return pl.pallas_call(
         unpack_body,
-        grid=(30,),
-        in_specs=[
-            pl.BlockSpec((UNIT, 128), lambda s: (s, 0)),
-            pl.BlockSpec((tail, 128), lambda s: (SPAN_ROW // tail, 0)),
-        ],
+        grid=(CHUNKS,),
+        in_specs=[pl.BlockSpec((CHUNK, 128), lambda s: (s, 0))],
         out_specs=[b for _, b in specs],
         out_shape=[jax.ShapeDtypeStruct(s, F32) for s, _ in specs],
         compiler_params=params(),
         cost_estimate=pl.CostEstimate(flops=0, bytes_accessed=27_000_000, transcendentals=0),
         name="unpack",
-    )(packed, packed)
+    )(packed)
 
 
 def shards(
@@ -985,42 +1014,37 @@
     n_blk = lax.axis_size("blk")
     short_x = short_input.reshape(short_input.shape[2:])
     short_cot = short_cotan.reshape(short_cotan.shape[2:])
-    vec = jnp.concatenate(
-        [
-            bias_query,
-            bias_value,
-            bias_point,
-            bias_unfold,
-            bias_output,
-            gain_first,
-            shift_first,
-            bias_outer,
-            gain_second,
-            shift_second,
-            bias_inner,
-            depth_kernel.reshape(-1),
-            bias_span,
-            jnp.zeros((24 * D - 21 * D - TAPS,), BF),
-        ]
-    ).reshape(24, D).astype(F32)
     perm, spread = (jnp.asarray(t) for t in tap_tables())
     xs = [long_input] + [
         lax.ppermute(long_input, "blk", [(i, (i + k) % n_blk) for i in range(n_blk)])
         for k in range(1, n_blk)
     ]
-    pre_consts = (vec, w_project, w_point, w_span, w_unfold, spread, perm)
-    ffn_consts = (vec, w_output, w_inner, w_outer)
+    span_t = w_span.T
+    pre_consts = (
+        bias_query, bias_value, bias_point, bias_span, bias_unfold, depth_kernel,
+        w_project, w_point, span_t, w_unfold, spread, perm,
+    )
+    ffn_consts = (
+        bias_output, gain_first, shift_first, bias_outer, gain_second, shift_second, bias_inner,
+        w_output, w_inner, w_outer,
+    )
     *short_kept, short_mixed = pre_call([short_x], pre_consts)
     *long_kept, long_mixed = pre_call(xs, pre_consts)
 
     tokens = (long_input.shape[0] + short_x.shape[0]) * short_x.shape[1]
     l_out, l_fig, l_mg, *joint, l_stat = ffn_call(
-        None, long_mixed, long_input, long_cotan, ffn_consts, (), tokens
+        None, 0, long_mixed, long_input, long_cotan, ffn_consts, (), tokens
     )
     s_out, s_fig, s_mg, left, right, s_stat = ffn_call(
-        live_slots, short_mixed, short_x, short_cot, ffn_consts, joint, tokens
+        live_slots,
+        short_x.shape[1],
+        *(a.reshape(-1, FFN_ROWS, D) for a in (short_mixed, short_x, short_cot)),
+        ffn_consts,
+        joint,
+        tokens,
     )
-    post_consts = (vec, w_point, w_span, spread, perm)
+    s_fig, s_mg = s_fig.reshape(short_x.shape), s_mg.reshape(short_x.shape)
+    post_consts = (depth_kernel, w_point, span_t, spread, perm)
     l_post = post_call(xs, l_mg, l_fig, long_kept, post_consts, (), tokens)
     (*joint, l_dkg, own), l_rest = l_post[:4], l_post[4:]
     far, (l_qt, l_ug, l_tg) = l_rest[: n_blk - 1], l_rest[n_blk - 1 :]
@@ -1052,7 +1076,7 @@
         depth,
         point,
         named["bias_point"],
-        span,
+        span.T,
         named["bias_span"],
         unfold,
         named["bias_unfold"],

time: 319 us -> 268 us (0.84)
  Pallas kernels: 294 us -> 257 us
  local copies, waits for them, and re-layouts: 16 us -> 2.99 us
    pallas_call x3, Pallas kernels: 85.9 us -> 61.2 us  [the longest x2 48.1 us: ffn_call(): pl.pallas_call(functools.partial(ffn_body, slot_rows if masked else 0), g...]
    pallas_call x2, Pallas kernels: 53.2 us -> 43.8 us  [post_call(): pl.pallas_call(functools.partial(post_body, len(xs)), grid=(count,), in_s...]
    concatenate x1 -> x0, local copies, waits for them, and re-layouts: 8.32 us -> none  [shards(): jnp.concatenate([bias_query, bias_value, bias_point, bias_unfold, bias_ou...]
    unnamed x14 -> x12, local copies, waits for them, and re-layouts: 6.21 us -> 2.99 us
  transfers between devices with their start and end apart: 6 -> 6, of which waited for: 0 -> 0; matrix products, arithmetic and copies ran while one was open for 4% -> 0% of each run, Pallas kernels for 33% -> 31%
where the time goes in v3:
time: 268 us
  Pallas kernels  257 us (96%)
  starting transfers between devices  6.29 us (2%)
  local copies, waits for them, and re-layouts  2.99 us (1%)
    pallas_call x1, Pallas kernels, weights_call(): pl.pallas_call(functools.partial(weights_body, remote), in_specs=[pl.Bloc...  105 us
    pallas_call x2, Pallas kernels, ffn_call(): pl.pallas_call(functools.partial(ffn_body, slot_rows if masked else 0), g...  48.1 us
    pallas_call x2, Pallas kernels, post_call(): pl.pallas_call(functools.partial(post_body, len(xs)), grid=(count,), in_s...  43.8 us
    pallas_call x2, Pallas kernels, pre_call(): pl.pallas_call(functools.partial(pre_body, len(xs)), grid=(count,), in_sp...  40.3 us
    pallas_call x1, Pallas kernels, unpack_call(): pl.pallas_call(unpack_body, grid=(CHUNKS,), in_specs=[pl.BlockSpec((CHUNK...  13.1 us
    pallas_call x1, Pallas kernels, end_call(): pl.pallas_call(functools.partial(end_body, 1 + len(far)), grid=(count,),...  6.74 us
  transfers between devices with their start and end apart: 6, of which 0 were waited for; matrix products, arithmetic and copies ran while one was open for 0% of the time, Pallas kernels for 31%

profile of v3, /device:TPU:1, one launch (start us, length us, event | category | flops | bytes accessed | tf_op | source)
XLA Modules:
  0.0 267.9 jit_solution(6049897663607027617)
XLA Ops:
  0.7 0.1 collective-permute-start.2
  0.8 2.7 collective-permute-start.1
  3.4 1.3 collective-permute-start
  5.4 24.9 %pre_short.1 = (bf16[8,128,384]{2,1,0:T(8,128)(2,1)}, bf16[8,128,384]{2,1,0:T(8,128)(2,1)}, bf16[8,128,384]{2,1,0:T(8,128)(2,1)}, bf16[8,3,256,128]{3,2,1,0:T(8,...) custom-call(bf16[8,128,768]{2,1,0:T(8,128)(2,1)} %bitcast.11, ...), custom_call_target="tpu_custom_call" | custom-call | flops 6144000000 | bytes 20000000 | tf_op jit(solution)/shard_map/pre_short/pallas_call | solution.py:232
  30.4 0.0 copy-start.4
  30.4 0.8 copy-done.3
  31.2 0.2 copy-done.4
  31.3 0.8 copy-done.5
  32.2 15.4 %pre_long.1 = (bf16[3,128,384]{2,1,0:T(8,128)(2,1)}, bf16[3,512,384]{2,1,0:T(8,128)(2,1)}, bf16[3,512,384]{2,1,0:T(8,128)(2,1)}, bf16[3,3,1024,128]{3,2,1,0:T(8,...) custom-call(bf16[3,128,768]{2,1,0:T(8,128)(2,1)} %refs_0_.4, ...), custom_call_target="tpu_custom_call" | custom-call | flops 2304000000 | bytes 20000000 | tf_op jit(solution)/shard_map/pre_long/pallas_call | solution.py:232
  47.6 17.7 %ffn_long.1 = (bf16[3,128,768]{2,1,0:T(8,128)(2,1)}, f32[3,128,768]{2,1,0:T(8,128)}, bf16[3,128,768]{2,1,0:T(8,128)(2,1)}, bf16[3072,1408]{1,0:T(8,128)(2,1)}, b...) custom-call(bf16[3,128,768]{2,1,0:T(8,128)(2,1)} %get-tuple-element.91.refs_0_, bf16[3,128,768]{2,1,0:T(8,128)(2,1)} %refs_0_.4, ...), custom_call_target="tpu_custom_call" | custom-call | flops 4608000000 | bytes 30000000 | tf_op jit(solution)/shard_map/ffn_long/pallas_call | solution.py:355
  65.3 14.7 %post_long.1 = (bf16[896,1408]{1,0:T(8,128)(2,1)}, bf16[1408,768]{1,0:T(8,128)(2,1)}, f32[72,768]{1,0:T(8,128)}, f32[3,128,768]{2,1,0:T(8,128)}, bf16[3,144,768]...) custom-call(bf16[3,128,768]{2,1,0:T(8,128)(2,1)} %refs_0_.4, ...), custom_call_target="tpu_custom_call" | custom-call | flops 3840000000 | bytes 30000000 | tf_op jit(solution)/shard_map/post_long/pallas_call | solution.py:535
  80.0 0.4 collective-permute-start.4
  80.5 1.2 collective-permute-start.3
  81.7 0.6 collective-permute-start.5
  82.2 30.4 %ffn_short.1 = (bf16[4,256,768]{2,1,0:T(8,128)(2,1)}, f32[4,256,768]{2,1,0:T(8,128)}, bf16[4,256,768]{2,1,0:T(8,128)(2,1)}, bf16[3072,1408]{1,0:T(8,128)(2,1)}, ...) custom-call(s32[1,1]{1,0:T(1,128)S(6)} %copy.61.refs_0_, ...), custom_call_target="tpu_custom_call", output_to_operand_aliasing={{3}: (14, {}), {4}: (15, {})} | custom-call | flops 12288000000 | bytes 30000000 | tf_op jit(solution)/shard_map/ffn_short/pallas_call | solution.py:355
  112.6 29.0 %post_short.1 = (bf16[896,1408]{1,0:T(8,128)(2,1)}, bf16[1408,768]{1,0:T(8,128)(2,1)}, f32[72,768]{1,0:T(8,128)}, f32[8,128,768]{2,1,0:T(8,128)}, bf16[1408,1536]{1,0:T(8,128)(2,1)}) custom-call(bf16[8,128,768]{2,1,0:T(8,128)(2,1)} %bitcast.13, bf16[8,128,768]{2,1,0:T(8,128)(2,1)} %bitcast.23, ...), custom_call_target="tpu_custom_call", output_to_operand_aliasing={{0}: (18, {}), {1}: (19, {})} | custom-call | flops 10240000000 | bytes 30000000 | tf_op jit(solution)/shard_map/post_short/pallas_call | solution.py:535
  141.6 0.0 copy-start.2
  141.6 0.0 copy-start
  141.7 0.8 copy-done.2
  142.4 0.2 copy-done
  142.7 0.2 copy-done.1
  142.9 6.7 %end_long.1 = (f32[3,128,768]{2,1,0:T(8,128)}, bf16[1408,1536]{1,0:T(8,128)(2,1)}) custom-call(f32[3,128,768]{2,1,0:T(8,128)} %get-tuple-element.107.refs_0_, bf16[3,144,768]{2,1,0:T(8,128)(2,1)} %copy-done, bf16[3,128,768]{2,1,0:T(8,128)(2,1)} %copy-done.2, bf16[3,144,768]{2,1,0:T(8,128)(2,1)} %copy-done.1, ...), custom_call_target="tpu_custom_call", output_to_operand_aliasing={{1}: (9, {})} | custom-call | flops 921600000 | bytes 10000000 | tf_op jit(solution)/shard_map/end_long/pallas_call | solution.py:581
  149.6 105.0 %weights.1.block = bf16[35328,128]{1,0:T(8,128)(2,1)} custom-call(bf16[3072,1408]{1,0:T(8,128)(2,1)} %get-tuple-element.129.refs_0_, bf16[1408,6912]{1,0:T(8,128)(2,1)} %get-tuple-element.130.refs_1_, bf16[896,1408]{1,0:T(8,128)(2,1)} %get-tuple-element.131.refs_2_, bf16[1408,768]{1,0:T(8,128)(2,1)} %get-tuple-element.132.refs_3_, ...), custom_call_target="tpu_custom_call" | custom-call | flops 12872318976 | bytes 50000000 | tf_op jit(solution)/shard_map/weights/pallas_call | solution.py:873
  254.6 13.1 %unpack.1 = (f32[2,384,1536]{2,1,0:T(8,128)}, f32[2,1536,384]{2,1,0:T(8,128)}, f32[768,768]{1,0:T(8,128)}, f32[768,384]{1,0:T(8,128)}, f32[768,1152]{1,0:T(8,128...) custom-call(bf16[35328,128]{1,0:T(8,128)(2,1)} %weights.1.block), custom_call_target="tpu_custom_call" | custom-call | bytes 27000000 | tf_op jit(solution)/shard_map/unpack/pallas_call | solution.py:975
  (9 shorter events, 0.0 us)
Async XLA Ops:
  0.7 29.7 %collective-permute-start.2 = (bf16[3,128,768]{2,1,0:T(8,128)(2,1)}, bf16[3,128,768]{2,1,0:T(8,128)(2,1)S(1)}, u32[]{:S(2)}, u32[]{:S(2)}) collective-permute-start(bf16[3,128,768]{2,1,0:T(8,128)(2,1)} %refs_0_.4), channel_id=1, source_target_pairs={{0,3},{1,0},{2,1},{3,2},{4,7},{5,4},{6,5},{7,6},{8,11},{9,8},{10,9... | collective-permute-start | bytes 1769480 | tf_op jit(solution)/shard_map/ppermute | solution.py:1019
  0.8 29.6 %collective-permute-start.1 = (bf16[3,128,768]{2,1,0:T(8,128)(2,1)}, bf16[3,128,768]{2,1,0:T(8,128)(2,1)S(1)}, u32[]{:S(2)}, u32[]{:S(2)}) collective-permute-start(bf16[3,128,768]{2,1,0:T(8,128)(2,1)} %refs_0_.4), channel_id=1, source_target_pairs={{0,2},{1,3},{2,0},{3,1},{4,6},{5,7},{6,4},{7,5},{8,10},{9,11},{10,... | collective-permute-start | bytes 1769480 | tf_op jit(solution)/shard_map/ppermute | solution.py:1019
  3.4 26.9 %collective-permute-start = (bf16[3,128,768]{2,1,0:T(8,128)(2,1)}, bf16[3,128,768]{2,1,0:T(8,128)(2,1)S(1)}, u32[]{:S(2)}, u32[]{:S(2)}) collective-permute-start(bf16[3,128,768]{2,1,0:T(8,128)(2,1)} %refs_0_.4), channel_id=1, source_target_pairs={{0,1},{1,2},{2,3},{3,0},{4,5},{5,6},{6,7},{7,4},{8,9},{9,10},{10,1... | collective-permute-start | bytes 1769480 | tf_op jit(solution)/shard_map/ppermute | solution.py:1019
  30.3 0.8 copy-start.3
  30.4 1.0 copy-start.4
  31.3 0.8 copy-start.5
  80.0 61.6 %collective-permute-start.4 = (bf16[3,128,768]{2,1,0:T(8,128)(2,1)}, bf16[3,128,768]{2,1,0:T(8,128)(2,1)S(1)}, u32[]{:S(2)}, u32[]{:S(2)}) collective-permute-start(bf16[3,128,768]{2,1,0:T(8,128)(2,1)} %get-tuple-element.109), channel_id=1, source_target_pairs={{0,2},{1,3},{2,0},{3,1},{4,6},{5,7},{6,4},{7,5},{8,10},{9,11},{10,... | collective-permute-start | bytes 1769480 | tf_op jit(solution)/shard_map/ppermute | solution.py:1052
  80.5 61.2 %collective-permute-start.3 = (bf16[3,144,768]{2,1,0:T(8,128)(2,1)}, bf16[3,144,768]{2,1,0:T(8,128)(2,1)S(1)}, u32[]{:S(2)}, u32[]{:S(2)}) collective-permute-start(bf16[3,144,768]{2,1,0:T(8,128)(2,1)} %get-tuple-element.108), channel_id=1, source_target_pairs={{0,3},{1,0},{2,1},{3,2},{4,7},{5,4},{6,5},{7,6},{8,11},{9,8},{10,9... | collective-permute-start | bytes 1990664 | tf_op jit(solution)/shard_map/ppermute | solution.py:1052
  81.7 60.0 %collective-permute-start.5 = (bf16[3,144,768]{2,1,0:T(8,128)(2,1)}, bf16[3,144,768]{2,1,0:T(8,128)(2,1)S(1)}, u32[]{:S(2)}, u32[]{:S(2)}) collective-permute-start(bf16[3,144,768]{2,1,0:T(8,128)(2,1)} %get-tuple-element.110), channel_id=1, source_target_pairs={{0,1},{1,2},{2,3},{3,0},{4,5},{5,6},{6,7},{7,4},{8,9},{9,10},{10,1... | collective-permute-start | bytes 1990664 | tf_op jit(solution)/shard_map/ppermute | solution.py:1052
  141.6 0.8 copy-start.2
  141.6 1.0 copy-start
  141.7 1.2 copy-start.1
